TPU v7x, 128 devices: a whole 4x4x4 slice. The times are simulated.
128 devices in a mesh: grp: 8 (over x, core), blk: 16 (over y, z).
Axes of the slice: x: 4, y: 4, z: 4, core: 2. Of those that a mesh axis runs over, the one named last changes fastest.
Arguments:
- stamps: float32 [128, 128, 64, 128], P(('grp', 'blk')), may hold values from -1 to 1
- stamp_target: int32 [128, 128, 128], P(('grp', 'blk')), may hold values from 0 to 4095
- pair_counts: int32 [128, 128], P(('grp', 'blk')), may hold values from 0 to 128, as said below
- conductance: float32 [8, 32768], P(None, ('grp', 'blk')), may hold values from 4 to 12
- block_cols: int32 [16, 32768], P(None, ('grp', 'blk')), may hold values from 0 to 32767, as said below
- newton_residual: float32 [8, 32768], P(None, ('grp', 'blk')), may hold values from -30 to 30
Outputs:
- update: float32 [8, 32768], P(None, ('grp', 'blk'))
- jacobian_blocks: float32 [16, 8, 8, 32768], P(None, None, None, ('grp', 'blk'))
- preconditioned_rhs: float32 [8, 32768], P(None, ('grp', 'blk'))
Inputs may be any that keep to these rules, and one draw needn't show every extreme that they name: `stamp_target`: A stamp's target is its block slot times 256 plus its block row local to the owner. `pair_counts`: every device sends exactly 128 live blocks to itself and exactly 128 to the next device in the order of grp+blk (the last device to the first), and at most 32 to every other owner; one owner drawn from the seed receives exactly 32 from every device other than itself and the device before it. `block_cols`: slot 0 of block row n names n itself; slots 1 to 7 name rows of the same group of 4096 rows as n; over the 256 block rows of one device, the slots from 8 on name rows owned by each device exactly 16 times.
All inputs are finite; a program needn't handle non-finite values.
Results may differ from a plain program's by a relative error of at most 0.0003.
Values sent between devices are 32-bit elements; how exact they have to be, the bound alone decides.
A program may use at most 128 MiB of HBM per device.

v0:
```python
import jax
import jax.numpy as jnp
from jax import lax
from jax.sharding import Mesh
from jax.sharding import PartitionSpec as P

K = 16
KRYLOV = 5
SWEEPS = 2
GRP = ("grp_0", "grp_1")
BLK = ("blk_0", "blk_1")
GRP_BLK = ("grp_0", "grp_1", "blk_0", "blk_1")


EPS = 1e-06


def sent_together(arrays, axis, split_dim, concat_dim, along):
    columns = [a.reshape(*a.shape[:along], -1) for a in arrays]
    both = jnp.concatenate(columns, axis=along)
    result, at, done = (
        lax.all_to_all(both, axis, split_axis=split_dim, concat_axis=concat_dim, tiled=True),
        0,
        [],
    )
    for a, column in zip(arrays, columns):
        piece = result[..., at : at + column.shape[along]]
        done.append(piece.reshape(*piece.shape[:along], *a.shape[along:]))
        at += column.shape[along]
    return tuple(done)


def passed_along(block, axis, distance):
    devices = range(lax.axis_size(axis))
    route = [((i - distance) % len(devices), i) for i in devices]
    return lax.ppermute(block, axis, route)


def in_order(parts, dim):
    dims = list(parts.shape[1:])
    dims[dim] *= parts.shape[0]
    return jnp.moveaxis(parts, 0, dim).reshape(dims)


def copy_for_each(array, axis):
    length = lax.axis_size(axis)
    return lax.all_to_all(
        jnp.broadcast_to(array[None], (length, *array.shape)), axis, 0, 0, tiled=True
    )


def collect(array, axis, dim):
    return in_order(copy_for_each(array, axis), dim)


def all_blocks(array, axes, sequence):
    parts = array[None]
    for k in sequence:
        parts = lax.all_gather(parts, axes[k], axis=0, tiled=True)
    held = [lax.axis_size(axes[k]) for k in reversed(sequence)]
    parts = parts.reshape(*held, *array.shape)
    turned = sorted(range(len(sequence)), key=lambda place: sequence[len(sequence) - 1 - place])
    return parts.transpose(*turned, *range(len(sequence), parts.ndim)).reshape(-1, *array.shape)


def gathered_by_axis(array, axes, sequence, dim):
    return in_order(all_blocks(array, axes, sequence), dim)


def by_axis(array, axes):
    for axis in axes:
        array = lax.psum(array, axis)
    return array


def invert_blocks(diag):
    size = diag.shape[0]
    eye_mat = jnp.eye(size, dtype=jnp.float32)[:, :, None]
    inverse = eye_mat * jnp.ones_like(diag[:1])
    work = diag
    for pivot_row in range(size):
        scale = 1.0 / work[pivot_row, pivot_row]
        top_work = work[pivot_row] * scale
        top_inverse = inverse[pivot_row] * scale
        factor = work[:, pivot_row]
        work = work - factor[:, None, :] * top_work[None]
        inverse = inverse - factor[:, None, :] * top_inverse[None]
        work = work.at[pivot_row].set(top_work)
        inverse = inverse.at[pivot_row].set(top_inverse)
    return inverse


def solve_small(matrix, rhs_vector):
    count = matrix.shape[0]
    work, vector = (matrix, rhs_vector)
    for pivot_row in range(count):
        scale = 1.0 / work[pivot_row, pivot_row]
        top_work = work[pivot_row] * scale
        top_rhs = vector[pivot_row] * scale
        factor = work[:, pivot_row]
        work = work - factor[:, None] * top_work[None, :]
        vector = vector - factor * top_rhs
        work = work.at[pivot_row].set(top_work)
        vector = vector.at[pivot_row].set(top_rhs)
    return vector


def block_apply(inverse, vector):
    return jnp.einsum("abn,bn->an", inverse, vector, precision=lax.Precision.HIGHEST)


def couple(jacobian, picked):
    return jnp.einsum("kabn,bkn->an", jacobian, picked, precision=lax.Precision.HIGHEST)


def add_stamps(summed, values, targets, counts, offset, local_rows):
    slots = values.shape[2]
    slot_ids = offset + jnp.arange(slots, dtype=jnp.int32)
    live = slot_ids[None, :] < counts
    masked = jnp.where(live[:, None, :], values, 0.0)
    index_pairs = jnp.stack([targets // local_rows, targets % local_rows], axis=2).astype(jnp.int32)
    numbers = lax.ScatterDimensionNumbers(
        update_window_dims=(1,), inserted_window_dims=(0, 2), scatter_dims_to_operand_dims=(0, 2)
    )
    return lax.scatter_add(summed, index_pairs, masked, numbers)


def local(stamps, stamp_target, pair_counts, conductance, block_cols, newton_residual):
    grp_count = lax.axis_size(GRP)
    blk_count = lax.axis_size(BLK)
    devices = grp_count * blk_count
    local_rows = conductance.shape[1]
    capacity = stamps.shape[3]
    summed = jnp.zeros((K, 64, local_rows), jnp.float32)
    front = capacity // 4
    got_values, got_target, got_counts = (
        lax.all_to_all(stamps[:, :, :, :front], GRP_BLK, split_axis=1, concat_axis=0, tiled=True),
        *sent_together((stamp_target[:, :, :front], pair_counts), GRP_BLK, 1, 0, 2),
    )
    summed = add_stamps(
        summed,
        got_values.reshape(devices, 64, front),
        got_target.reshape(devices, front),
        got_counts,
        0,
        local_rows,
    )
    my_index = lax.axis_index(GRP_BLK)
    next_index = (my_index + 1) % devices
    own_values = lax.dynamic_index_in_dim(stamps[0], my_index, 0, keepdims=False)[:, front:]
    own_target = lax.dynamic_index_in_dim(stamp_target[0], my_index, 0, keepdims=False)[front:]
    own_count = lax.dynamic_index_in_dim(pair_counts[0], my_index, 0, keepdims=True)
    next_values = lax.dynamic_index_in_dim(stamps[0], next_index, 0, keepdims=False)[:, front:]
    next_target = lax.dynamic_index_in_dim(stamp_target[0], next_index, 0, keepdims=False)[front:]
    next_count = lax.dynamic_index_in_dim(pair_counts[0], next_index, 0, keepdims=True)
    prior_values, prior_target, prior_count = passed_along(
        (next_values, next_target, next_count), GRP_BLK, 1
    )
    tail_values = jnp.stack([own_values, prior_values], axis=0)
    tail_target = jnp.stack([own_target, prior_target], axis=0)
    tail_counts = jnp.stack([own_count, prior_count], axis=0)
    summed = add_stamps(summed, tail_values, tail_target, tail_counts, front, local_rows)
    jacobian = summed.reshape(K, 8, 8, local_rows)
    identity = jnp.eye(8, dtype=jnp.float32)
    jacobian = jacobian.at[0].add(identity[:, :, None] * conductance[:, None, :])
    inverse = invert_blocks(jacobian[0])
    group_rows = local_rows * blk_count
    group_start = lax.axis_index(GRP) * group_rows
    slot_ids = jnp.arange(K, dtype=jnp.int32)[:, None]
    near = (block_cols >= group_start) & (block_cols < group_start + group_rows) & (slot_ids >= 1)
    local_cols = jnp.clip(block_cols - group_start, 0, group_rows - 1)
    rhs_field = -newton_residual
    beta = jnp.sqrt(by_axis(jnp.sum(rhs_field * rhs_field), GRP_BLK) + EPS)
    basis = [rhs_field / beta]
    search = []
    hess = jnp.zeros((KRYLOV + 1, KRYLOV), jnp.float32)
    for krylov_step in range(KRYLOV):
        precondition_vector = basis[krylov_step]
        result = block_apply(inverse, precondition_vector)
        for sweep_index in range(SWEEPS):
            grouped = collect(result, BLK, 1)
            precondition_picked = jnp.where(near[None], grouped[:, local_cols], 0.0)
            result = block_apply(
                inverse, precondition_vector - couple(jacobian, precondition_picked)
            )
        search.append(result)
        whole = gathered_by_axis(result, GRP_BLK, (0, 2, 3, 1), 1)
        picked = whole[:, block_cols]
        image = couple(jacobian, picked)
        partial_value = jnp.stack([jnp.sum(basis_vec * image) for basis_vec in basis])
        projections, squares = (
            by_axis(partial_value, GRP_BLK),
            by_axis(jnp.sum(image * image), GRP_BLK),
        )
        for index_i, basis_vec in enumerate(basis):
            image = image - projections[index_i] * basis_vec
        length = jnp.sqrt(squares - jnp.sum(projections * projections) + EPS)
        hess = hess.at[: krylov_step + 1, krylov_step].set(projections)
        hess = hess.at[krylov_step + 1, krylov_step].set(length)
        if krylov_step + 1 < KRYLOV:
            basis.append(image / length)
    normal = jnp.dot(hess.T, hess, precision=lax.Precision.HIGHEST)
    coef = solve_small(normal, beta * hess[0])
    update = coef[0] * search[0]
    for index_j in range(1, KRYLOV):
        update = update + coef[index_j] * search[index_j]
    return (update, jacobian, beta * search[0])


def solution(mesh):
    torus = Mesh(mesh.devices.reshape(4, 2, 4, 4), ("grp_0", "grp_1", "blk_0", "blk_1"))
    return jax.shard_map(
        local,
        mesh=torus,
        in_specs=(
            P(GRP_BLK, None, None, None),
            P(GRP_BLK, None, None),
            P(GRP_BLK, None),
            P(None, GRP_BLK),
            P(None, GRP_BLK),
            P(None, GRP_BLK),
        ),
        out_specs=(P(None, GRP_BLK), P(None, None, None, GRP_BLK), P(None, GRP_BLK)),
        check_vma=False,
    )
```

profile of v0, /device:TPU:1, one launch (start us, length us, event | category | flops | bytes accessed | tf_op | source)
XLA Modules:
  0.0 1028.3 jit_solution(8667777961732287962)
XLA Ops:
  78.8 18.1 %all-to-all-done.1 = f32[128,1,2048]{2,1,0:T(1,128)S(1)} async-done(((f32[128,1,2048]{2,1,0:T(1,128)}), f32[128,1,2048]{2,1,0:T(1,128)S(1)}, u32[]{:S(2)}, u32[]{:S(2)}) %all-to-all-start.1) | async-done | bytes 1048608 | tf_op jit(solution)/shard_map/all_to_all | solution.py:137
  103.9 23.3 %scatter_custom_fusion.1 = f32[4096,64]{1,0:T(8,128)S(1)} fusion(s32[4096]{0:T(1024)S(1)} %reshape.1985, f32[4096,64]{1,0:T(8,128)} %bitcast.629, f32[]{:T(128)} %constant.944.clone.1), kind=kCustom, calls=%fused_computation.43 | custom fusion | flops 262144 | bytes 1049088
  150.4 14.1 %gather_fusion = f32[4096,8]{1,0:T(8,128)} fusion(f32[8,4096]{0,1:T(8,128)S(1)} %bitcast.604, s32[4096]{0:T(1024)S(1)} %broadcast_clamp_fusion.1), kind=kCustom, calls=%fused_computation | custom fusion | bytes 278528 | tf_op jit(solution)/shard_map/gather | solution.py:182
  177.9 14.1 %gather_fusion.1 = f32[4096,8]{1,0:T(8,128)} fusion(f32[8,4096]{0,1:T(8,128)S(1)} %bitcast.605, s32[4096]{0:T(1024)S(1)} %broadcast_clamp_fusion.1), kind=kCustom, calls=%fused_computation.1 | custom fusion | bytes 278528 | tf_op jit(solution)/shard_map/gather | solution.py:182
  223.7 20.0 %all-gather.11.cloned.1.call-done = f32[128,8,256]{2,1,0:T(8,128)} async-done(((f32[64,8,256]{2,1,0:T(8,128)}), f32[128,8,256]{2,1,0:T(8,128)}) %all-gather.11.cloned.1.call-update) | async-done | bytes 1048592 | tf_op jit(solution)/shard_map/all_gather | solution.py:59
  253.6 16.5 %gather_fusion.2 = f32[4096,8]{1,0:T(8,128)S(1)} fusion(f32[8,32768]{0,1:T(8,128)} %bitcast.597, s32[4096]{0:T(1024)S(1)} %broadcast_clamp_fusion), kind=kCustom, calls=%fused_computation.2 | custom fusion | bytes 278528 | tf_op jit(solution)/shard_map/gather | solution.py:188
  316.4 14.1 %gather_fusion.3 = f32[4096,8]{1,0:T(8,128)} fusion(f32[8,4096]{0,1:T(8,128)S(1)} %bitcast.606, s32[4096]{0:T(1024)S(1)} %broadcast_clamp_fusion.1), kind=kCustom, calls=%fused_computation.3 | custom fusion | bytes 278528 | tf_op jit(solution)/shard_map/gather | solution.py:182
  343.6 14.1 %gather_fusion.4 = f32[4096,8]{1,0:T(8,128)} fusion(f32[8,4096]{0,1:T(8,128)S(1)} %bitcast.607, s32[4096]{0:T(1024)S(1)} %broadcast_clamp_fusion.1), kind=kCustom, calls=%fused_computation.4 | custom fusion | bytes 278528 | tf_op jit(solution)/shard_map/gather | solution.py:182
  378.8 10.8 %all_gather.66 = f32[64,8,256]{2,1,0:T(8,128)} all-gather(f32[16,8,256]{2,1,0:T(8,128)S(1)} %all_gather.65), channel_id=1, replica_groups=mesh['grp_0'=4,'grp_1'=2,'blk_0'=4,'blk_1'=4] {'blk_1'}, dimensions={0}, use_global_device_ids=true | all-gather | bytes 655360 | tf_op jit(solution)/shard_map/all_gather | solution.py:59
  389.7 23.2 %all-gather.13.cloned.1.call-done = f32[128,8,256]{2,1,0:T(8,128)} async-done(((f32[64,8,256]{2,1,0:T(8,128)}), f32[128,8,256]{2,1,0:T(8,128)}) %all-gather.13.cloned.1.call-update) | async-done | bytes 1048592 | tf_op jit(solution)/shard_map/all_gather | solution.py:59
  422.7 16.5 %gather_fusion.5 = f32[4096,8]{1,0:T(8,128)S(1)} fusion(f32[8,32768]{0,1:T(8,128)} %bitcast.598, s32[4096]{0:T(1024)S(1)} %broadcast_clamp_fusion), kind=kCustom, calls=%fused_computation.5 | custom fusion | bytes 278528 | tf_op jit(solution)/shard_map/gather | solution.py:188
  488.4 14.1 %gather_fusion.6 = f32[4096,8]{1,0:T(8,128)} fusion(f32[8,4096]{0,1:T(8,128)S(1)} %bitcast.608, s32[4096]{0:T(1024)S(1)} %broadcast_clamp_fusion.1), kind=kCustom, calls=%fused_computation.6 | custom fusion | bytes 278528 | tf_op jit(solution)/shard_map/gather | solution.py:182
  515.6 14.1 %gather_fusion.7 = f32[4096,8]{1,0:T(8,128)} fusion(f32[8,4096]{0,1:T(8,128)S(1)} %bitcast.609, s32[4096]{0:T(1024)S(1)} %broadcast_clamp_fusion.1), kind=kCustom, calls=%fused_computation.7 | custom fusion | bytes 278528 | tf_op jit(solution)/shard_map/gather | solution.py:182
  550.8 10.8 %all_gather.70 = f32[64,8,256]{2,1,0:T(8,128)} all-gather(f32[16,8,256]{2,1,0:T(8,128)S(1)} %all_gather.69), channel_id=1, replica_groups=mesh['grp_0'=4,'grp_1'=2,'blk_0'=4,'blk_1'=4] {'blk_1'}, dimensions={0}, use_global_device_ids=true | all-gather | bytes 655360 | tf_op jit(solution)/shard_map/all_gather | solution.py:59
  561.7 23.2 %all-gather.15.cloned.1.call-done = f32[128,8,256]{2,1,0:T(8,128)} async-done(((f32[64,8,256]{2,1,0:T(8,128)}), f32[128,8,256]{2,1,0:T(8,128)}) %all-gather.15.cloned.1.call-update) | async-done | bytes 1048592 | tf_op jit(solution)/shard_map/all_gather | solution.py:59
  594.7 16.5 %gather_fusion.8 = f32[4096,8]{1,0:T(8,128)S(1)} fusion(f32[8,32768]{0,1:T(8,128)} %bitcast.599, s32[4096]{0:T(1024)S(1)} %broadcast_clamp_fusion), kind=kCustom, calls=%fused_computation.8 | custom fusion | bytes 278528 | tf_op jit(solution)/shard_map/gather | solution.py:188
  661.5 14.1 %gather_fusion.9 = f32[4096,8]{1,0:T(8,128)} fusion(f32[8,4096]{0,1:T(8,128)S(1)} %bitcast.610, s32[4096]{0:T(1024)S(1)} %broadcast_clamp_fusion.1), kind=kCustom, calls=%fused_computation.9 | custom fusion | bytes 278528 | tf_op jit(solution)/shard_map/gather | solution.py:182
  688.7 14.1 %gather_fusion.10 = f32[4096,8]{1,0:T(8,128)} fusion(f32[8,4096]{0,1:T(8,128)S(1)} %bitcast.611, s32[4096]{0:T(1024)S(1)} %broadcast_clamp_fusion.1), kind=kCustom, calls=%fused_computation.10 | custom fusion | bytes 278528 | tf_op jit(solution)/shard_map/gather | solution.py:182
  723.9 10.8 %all_gather.74 = f32[64,8,256]{2,1,0:T(8,128)} all-gather(f32[16,8,256]{2,1,0:T(8,128)S(1)} %all_gather.73), channel_id=1, replica_groups=mesh['grp_0'=4,'grp_1'=2,'blk_0'=4,'blk_1'=4] {'blk_1'}, dimensions={0}, use_global_device_ids=true | all-gather | bytes 655360 | tf_op jit(solution)/shard_map/all_gather | solution.py:59
  735.4 22.6 %all-gather.17.cloned.1.call-done = f32[128,8,256]{2,1,0:T(8,128)} async-done(((f32[64,8,256]{2,1,0:T(8,128)}), f32[128,8,256]{2,1,0:T(8,128)}) %all-gather.17.cloned.1.call-update) | async-done | bytes 1048592 | tf_op jit(solution)/shard_map/all_gather | solution.py:59
  767.8 16.5 %gather_fusion.11 = f32[4096,8]{1,0:T(8,128)S(1)} fusion(f32[8,32768]{0,1:T(8,128)} %bitcast.600, s32[4096]{0:T(1024)S(1)} %broadcast_clamp_fusion), kind=kCustom, calls=%fused_computation.11 | custom fusion | bytes 278528 | tf_op jit(solution)/shard_map/gather | solution.py:188
  837.2 14.1 %gather_fusion.12 = f32[4096,8]{1,0:T(8,128)} fusion(f32[8,4096]{0,1:T(8,128)S(1)} %bitcast.612, s32[4096]{0:T(1024)S(1)} %broadcast_clamp_fusion.1), kind=kCustom, calls=%fused_computation.12 | custom fusion | bytes 278528 | tf_op jit(solution)/shard_map/gather | solution.py:182
  865.4 14.1 %gather_fusion.13 = f32[4096,8]{1,0:T(8,128)} fusion(f32[8,4096]{0,1:T(8,128)S(1)} %bitcast.603, s32[4096]{0:T(1024)S(1)} %broadcast_clamp_fusion.1), kind=kCustom, calls=%fused_computation.13 | custom fusion | bytes 278528 | tf_op jit(solution)/shard_map/gather | solution.py:182
  944.4 16.5 %gather_fusion.14 = f32[4096,8]{1,0:T(8,128)S(1)} fusion(f32[8,32768]{0,1:T(8,128)} %bitcast.596, s32[4096]{0:T(1024)S(1)} %broadcast_clamp_fusion), kind=kCustom, calls=%fused_computation.14 | custom fusion | bytes 278528 | tf_op jit(solution)/shard_map/gather | solution.py:188
  (360 shorter events, 611.5 us)
Async XLA Ops:
  8.5 59.9 %collective-permute-start.1 = (s32[1]{0:T(128)}, s32[1]{0:T(128)}, u32[]{:S(2)}, u32[]{:S(2)}) collective-permute-start(s32[1]{0:T(128)} %bitcast.71), channel_id=1, source_target_pairs={{127,0},{0,1},{1,2},{2,3},{3,4},{4,5},{5,6},{6,7},{7,8},{8,9},{9,1... | collective-permute-start | bytes 20 | tf_op jit(solution)/shard_map/ppermute | solution.py:36
  11.9 66.9 %collective-permute-start.2 = (f32[64,96]{1,0:T(8,128)S(1)}, f32[64,96]{1,0:T(8,128)S(1)}, u32[]{:S(2)}, u32[]{:S(2)}) collective-permute-start(f32[64,96]{1,0:T(8,128)S(1)} %slice.984), channel_id=1, source_target_pairs={{127,0},{0,1},{1,2},{2,3},{3,4},{4,5},{5,6},{6,7},{7,8},{8,9},{9,1... | collective-permute-start | bytes 73736 | tf_op jit(solution)/shard_map/ppermute | solution.py:36
  14.3 55.6 %collective-permute-start = (s32[96]{0:T(128)S(1)}, s32[96]{0:T(128)S(1)}, u32[]{:S(2)}, u32[]{:S(2)}) collective-permute-start(s32[96]{0:T(128)S(1)} %slice_bitcast_fusion.6), channel_id=1, source_target_pairs={{127,0},{0,1},{1,2},{2,3},{3,4},{4,5},{5,6},{6,7},{7,8},{8,9},{9,1... | collective-permute-start | bytes 1160 | tf_op jit(solution)/shard_map/ppermute | solution.py:36
  18.0 52.0 %all-to-all-start = ((s32[1,128,33]{2,0,1:T(1,128)}), s32[1,128,33]{2,0,1:T(1,128)S(1)}, u32[]{:S(2)}, u32[]{:S(2)}) async-start(s32[1,128,33]{2,0,1:T(1,128)} %copy.71), calls=%async_computation | async-start | bytes 131072 | tf_op jit(solution)/shard_map/all_to_all | solution.py:22
  46.4 21.9 %copy-start.1 = (f32[8,256]{1,0:T(8,128)S(1)}, f32[8,256]{1,0:T(8,128)}, u32[]{:S(2)}) copy-start(f32[8,256]{1,0:T(8,128)} %param.81) | copy-start | bytes 24580
  46.4 21.9 %copy-start.3 = (s32[16,256]{1,0:T(8,128)S(1)}, s32[16,256]{1,0:T(8,128)}, u32[]{:S(2)}) copy-start(s32[16,256]{1,0:T(8,128)} %param.80) | copy-start | bytes 49156
  57.9 20.2 %copy-start.5 = (s32[2]{0:T(128)S(1)}, s32[2]{0:T(128)}, u32[]{:S(2)}) copy-start(s32[2]{0:T(128)} %constant.981) | copy-start | bytes 28
  57.9 20.3 %copy-start.4 = (s32[2]{0:T(128)S(1)}, s32[2]{0:T(128)}, u32[]{:S(2)}) copy-start(s32[2]{0:T(128)} %constant.984) | copy-start | bytes 28
  70.0 26.9 %all-to-all-start.1 = ((f32[128,1,2048]{2,1,0:T(1,128)}), f32[128,1,2048]{2,1,0:T(1,128)S(1)}, u32[]{:S(2)}, u32[]{:S(2)}) async-start(f32[128,1,2048]{2,1,0:T(1,128)} %reshape.2102), calls=%async_computation.1 | async-start | bytes 2097152 | tf_op jit(solution)/shard_map/all_to_all | solution.py:137
  137.1 0.7 copy-start.2
  138.0 823.5 %copy-start = (f32[16,8,8,256]{3,2,1,0:T(8,128)}, f32[16,8,8,256]{3,2,1,0:T(8,128)S(1)}, u32[]{:S(2)}) copy-start(f32[16,8,8,256]{3,2,1,0:T(8,128)S(1)} %get-tuple-element.493) | copy-start | bytes 3145732
  139.6 10.1 all-to-all-start.2
  143.1 100.6 %all-gather.11.cloned.1.call-start = ((), (), s32[]{:S(2)}) async-start(), calls=%async_computation.12 | async-start | bytes 1572864 | tf_op jit(solution)/shard_map/all_gather | solution.py:59
  223.6 189.3 %all-gather.13.cloned.1.call-start = ((), (), s32[]{:S(2)}) async-start(), calls=%async_computation.13 | async-start | bytes 1572864 | tf_op jit(solution)/shard_map/all_gather | solution.py:59
  389.6 195.3 %all-gather.15.cloned.1.call-start = ((), (), s32[]{:S(2)}) async-start(), calls=%async_computation.14 | async-start | bytes 1572864 | tf_op jit(solution)/shard_map/all_gather | solution.py:59
  561.7 196.3 %all-gather.17.cloned.1.call-start = ((), (), s32[]{:S(2)}) async-start(), calls=%async_computation.15 | async-start | bytes 1572864 | tf_op jit(solution)/shard_map/all_gather | solution.py:59
  826.5 10.1 all-to-all-start.10
  854.6 10.1 all-to-all-start.11
  858.1 76.5 %all-gather.19.cloned.1.call-start = ((), (), s32[]{:S(2)}) async-start(), calls=%async_computation.16 | async-start | bytes 1572864 | tf_op jit(solution)/shard_map/all_gather | solution.py:59
  881.4 31.3 %copy-start.8 = (s32[2]{0:T(128)S(1)}, s32[2]{0:T(128)}, u32[]{:S(2)}) copy-start(s32[2]{0:T(128)} %constant.972.clone.1) | copy-start | bytes 28
  881.4 31.9 %copy-start.7 = (s32[2]{0:T(128)S(1)}, s32[2]{0:T(128)}, u32[]{:S(2)}) copy-start(s32[2]{0:T(128)} %constant.973.clone.1) | copy-start | bytes 28
  881.4 32.6 %copy-start.6 = (s32[2]{0:T(128)S(1)}, s32[2]{0:T(128)}, u32[]{:S(2)}) copy-start(s32[2]{0:T(128)} %constant.974.clone.1) | copy-start | bytes 28
Sparse Core Ops, SparseCore 0:
  223.7 19.9 all-gather.10
  389.7 23.1 all-gather.12
  561.8 23.1 all-gather.14
  734.8 23.1 all-gather.16
  911.5 23.1 all-gather.18
where the time goes:
time: 1040 us; the launch traced here: 1030 us
  blocking collectives  409 us (39%)
  local copies, waits for them, and re-layouts  323 us (31%)
  waiting for transfers between devices  134 us (13%)
  other arithmetic  97.2 us (9%)
  starting transfers between devices  34.1 us (3%)
  between operations  30.3 us (3%)
    psum x24, blocking collectives, by_axis(): array = lax.psum(array, axis)  196 us
    all_gather x15, blocking collectives, all_blocks(): parts = lax.all_gather(parts, axes[k], axis=0, tiled=True)  146 us
    gather x10, local copies, waits for them, and re-layouts, local(): precondition_picked = jnp.where(near[None], grouped[:, local_cols], 0.0)  141 us
    all_gather x5, waiting for transfers between devices, all_blocks(): parts = lax.all_gather(parts, axes[k], axis=0, tiled=True)  97.8 us
    gather x5, local copies, waits for them, and re-layouts, local(): picked = whole[:, block_cols]  82.7 us
    all_to_all x7, blocking collectives, copy_for_each(): lax.all_to_all(jnp.broadcast_to(array[None], (length, *array.shape)), axi...  67.6 us
    transpose x5, local copies, waits for them, and re-layouts, all_blocks(): parts.transpose(*turned, *range(len(sequence), parts.ndim))  49.1 us
    unnamed x26, other arithmetic  42.9 us
  transfers between devices with their start and end apart: 13, of which 9 were waited for; matrix products, arithmetic and copies ran while one was open for 3% of the time, Pallas kernels for 0%

commit v1 on v0

v1 whole, which is shorter than its diff:
```python
import functools
import jax
import jax.numpy as jnp
from jax import lax
from jax.experimental import pallas as pl
from jax.experimental.pallas import tpu as pltpu
from jax.sharding import PartitionSpec as P

K = 16
KRYLOV = 5
NBR = 256
NGRP = 8
NBLK = 16
DEVICES = 128
LANES = 128
EPS = 1e-06
MESH = pl.DeviceIdType.MESH
AXES = ("grp", "blk")


def bf(x):
    return x.astype(jnp.float32).astype(jnp.bfloat16)


def iota(shape, dim):
    return lax.broadcasted_iota(jnp.int32, shape, dim)


def lane_pick(table, index):
    return jnp.take_along_axis(table, index, axis=1, mode="promise_in_bounds")


def fold_rows(parts):
    row = iota(parts[0].shape, 0)
    step = 1
    while len(parts) > 1:
        even = (row & step) == 0
        merged = []
        for first, second in zip(parts[0::2], parts[1::2]):
            kept = jnp.where(even, first, second)
            moved = jnp.where(even, second, first)
            merged.append(kept + pltpu.roll(moved, step, 0))
        parts = merged
        step *= 2
    return parts[0]


def block_mul(blocks, vector):
    return fold_rows([blocks[a] * vector for a in range(8)])


def small_solve(gram, scales):
    inv = [1.0 / s for s in scales] + [1.0]
    sc = list(scales) + [1.0]
    n = KRYLOV + 1
    g = [[None] * n for _ in range(n)]
    for l in range(n):
        for m in range(l + 1):
            val = gram[l][m] * sc[l] * sc[m]
            g[l][m] = val
            g[m][l] = val
    beta = jnp.sqrt(gram[0][0] + EPS)
    basis = [[inv[0] / beta]]
    hess = []
    for j in range(KRYLOV):
        b = basis[j]
        w = [None] * (j + 2)
        for l in range(j + 1):
            w[l] = b[l] if w[l] is None else w[l] + b[l]
            w[l + 1] = b[l] * inv[l + 1]
        gw = []
        for l in range(j + 2):
            t = g[l][0] * w[0]
            for m in range(1, j + 2):
                t = t + g[l][m] * w[m]
            gw.append(t)
        column = []
        for i in range(j + 1):
            t = basis[i][0] * gw[0]
            for l in range(1, i + 1):
                t = t + basis[i][l] * gw[l]
            column.append(t)
        for i in range(j + 1):
            for l in range(i + 1):
                w[l] = w[l] - column[i] * basis[i][l]
        sq = None
        for l in range(j + 2):
            t = g[l][0] * w[0]
            for m in range(1, j + 2):
                t = t + g[l][m] * w[m]
            sq = t * w[l] if sq is None else sq + t * w[l]
        length = jnp.sqrt(jnp.maximum(sq, 0.0) + EPS)
        column.append(length)
        hess.append(column)
        scale = 1.0 / length
        basis.append([x * scale for x in w])
    work = [[None] * KRYLOV for _ in range(KRYLOV)]
    for p in range(KRYLOV):
        for q in range(p + 1):
            t = hess[p][0] * hess[q][0]
            for i in range(1, q + 2):
                t = t + hess[p][i] * hess[q][i]
            work[p][q] = t
            work[q][p] = t
    vec = [beta * hess[p][0] for p in range(KRYLOV)]
    for p in range(KRYLOV):
        scale = 1.0 / work[p][p]
        top = [x * scale for x in work[p]]
        tv = vec[p] * scale
        for q in range(KRYLOV):
            if q == p:
                continue
            f = work[q][p]
            work[q] = [x - f * y for x, y in zip(work[q], top)]
            vec[q] = vec[q] - f * tv
        work[p] = top
        vec[p] = tv
    out = []
    for l in range(KRYLOV):
        t = None
        for j in range(l, KRYLOV):
            x = vec[j] * basis[j][l]
            t = x if t is None else t + x
        out.append(t * sc[l])
    return out


def krylov_kernel(jac, dinv, res, cols, upd, pre,
                  buf_a, buf_b, buf_c, fsrc, fbuf, req_src, req, nsrc, nbuf, rsrc, rbuf,
                  us, ss, gp, sig, pidx, lst, fpk,
                  sem_sa, sem_sb, sem_sc, sem_sf, sem_sn, sem_ra, sem_rb, sem_rc, sem_rf, sem_rn):
    g, i = lax.axis_index("grp"), lax.axis_index("blk")
    me = g * NBLK + i

    def mate(o):
        return (g, lax.rem(i + o, NBLK))

    def peer(o):
        return (lax.rem(g + o, NGRP), i)

    def far_dev(t):
        return lax.rem(g + 1 + t // NBLK, NGRP), lax.rem(i + t, NBLK)

    barrier = pltpu.get_barrier_semaphore()

    def greet(o, c):
        d = lax.rem(me + o, DEVICES)
        pl.semaphore_signal(barrier, inc=1, device_id=(d // NBLK, lax.rem(d, NBLK)), device_id_type=MESH)
        return c

    lax.fori_loop(1, DEVICES, greet, 0)

    owner_row = iota((DEVICES, NBR), 0)
    upper = bf(iota((NBR, NBR), 0) < iota((NBR, NBR), 1))
    before = jnp.zeros((DEVICES, 1), jnp.float32)
    wanted = jnp.zeros((DEVICES, LANES), jnp.float32)
    listed = jnp.zeros((8, NBR), jnp.float32)
    nt = (((1,), (1,)), ((), ()))
    for k in range(8):
        col = cols[8 + k : 9 + k, :]
        owner = lax.shift_right_logical(col, 8)
        row = col & 255
        hit = owner_row == owner
        one = jnp.where(hit, 1.0, 0.0)
        ahead = jnp.dot(one.astype(jnp.bfloat16), upper, preferred_element_type=jnp.float32) + before
        rank = jnp.sum(jnp.where(hit, ahead, 0.0), axis=0, keepdims=True).astype(jnp.int32)
        before = before + jnp.sum(one, axis=1, keepdims=True)
        place = owner * 16 + rank
        pidx[k : k + 1, :] = place
        rowf = row.astype(jnp.float32)
        ranked = jnp.where((owner_row & 15) == rank, rowf, 0.0).astype(jnp.bfloat16)
        wanted = wanted + lax.dot_general(one.astype(jnp.bfloat16), ranked, nt, preferred_element_type=jnp.float32)
        mine = bf(iota((NBR, NBR), 0) == place - g * NBR)
        rows8 = jnp.broadcast_to(rowf, (8, NBR)).astype(jnp.bfloat16)
        listed = listed + lax.dot_general(rows8, mine, nt, preferred_element_type=jnp.float32)
    req_src[...] = wanted.astype(jnp.int32)
    lst[...] = (lax.shift_right_logical(iota((8, NBR), 1), 4) * NBR + listed.astype(jnp.int32))[0:1]

    pl.semaphore_wait(barrier, DEVICES - 1)

    def ask(t, c):
        dg, di = far_dev(t)
        d = dg * NBLK + di
        pltpu.make_async_remote_copy(
            src_ref=req_src.at[pl.ds(d, 1)], dst_ref=req.at[pl.ds(me, 1)], send_sem=sem_sn.at[2], recv_sem=sem_rn.at[2],
            device_id=(dg, di), device_id_type=MESH).start()
        return c

    lax.fori_loop(0, 112, ask, 0)
    us[...] = jnp.zeros_like(us)
    us[0] = -res[...]
    rsrc[...] = jnp.zeros_like(rsrc)

    def whole(ref, rows, send, recv):
        return pltpu.make_async_remote_copy(
            src_ref=ref.at[pl.ds(0, rows)], dst_ref=ref.at[pl.ds(0, rows)], send_sem=send, recv_sem=recv,
            device_id=mate(1), device_id_type=MESH)

    asked = whole(req, 112, sem_sn.at[2], sem_rn.at[2])
    asked.wait_recv()
    asked.wait_send()

    order = (10, 9, 11, 6, 14, 5, 7, 13, 15, 2, 8, 1, 3, 4, 12)

    def spread(buf, send, recv):
        for o in order:
            y, z = i // 4, lax.rem(i, 4)
            to = lax.rem(y + o // 4, 4) * 4 + lax.rem(z + o % 4, 4)
            pltpu.make_async_remote_copy(
                src_ref=buf.at[i], dst_ref=buf.at[i], send_sem=send, recv_sem=recv,
                device_id=(g, to), device_id_type=MESH).start()

    def near_pick(buf):
        picked = []
        for q in range(16):
            if q < 14:
                idx = cols[1 + q // 2 : 2 + q // 2, q % 2 * LANES : (q % 2 + 1) * LANES] - g * (NBLK * NBR)
            else:
                idx = lst[:, (q - 14) * LANES : (q - 13) * LANES]
            idx = jnp.broadcast_to(idx, (8, LANES))
            lo, hi = idx & 127, lax.shift_right_logical(idx, 7)
            acc = jnp.zeros((8, LANES), jnp.float32)
            for v in range(32):
                acc = jnp.where(hi == v, lane_pick(buf[v // 2, :, v % 2 * LANES : (v % 2 + 1) * LANES], lo), acc)
            picked.append(acc)
        return picked

    def far_place(q):
        idx = jnp.broadcast_to(pidx[q // 2 : q // 2 + 1, q % 2 * LANES : (q % 2 + 1) * LANES], (8, LANES))
        return idx & 127, lax.shift_right_logical(idx, 7)

    def add_slot(acc, k, picked):
        return [x + jac[k, a] * picked for a, x in enumerate(acc)]

    def joined(first, second):
        return jnp.concatenate([first, second], axis=1)

    def near_couple(buf):
        picked = near_pick(buf)
        acc = [jnp.zeros((8, NBR), jnp.float32)] * 8
        for k in range(7):
            acc = add_slot(acc, 1 + k, joined(picked[2 * k], picked[2 * k + 1]))
        for k in range(8):
            got = []
            for h in range(2):
                lo, hi = far_place(2 * k + h)
                x = jnp.zeros((8, LANES), jnp.float32)
                for v in range(2):
                    x = jnp.where(hi == 2 * g + v, lane_pick(picked[14 + v], lo), x)
                got.append(x)
            acc = add_slot(acc, 8 + k, joined(*got))
        return fold_rows(acc)

    lane16 = iota((8, LANES), 1) & 15
    lane_group = lax.shift_right_logical(iota((8, LANES), 1), 4)
    turn = iota((8, LANES), 0) * 16 + lane16

    def step(j, carry):
        slot = lax.rem(j, 2)
        u = us[j]
        z = block_mul(dinv, u)
        buf_a[i, :, 0:NBR] = z
        sq = u * u
        buf_a[i, :, NBR : NBR + LANES] = sq[:, :LANES] + sq[:, LANES:]
        spread(buf_a, sem_sa, sem_ra)
        dots = []
        for l in range(6):
            t = u * us[l]
            dots.append(t[:, :LANES] + t[:, LANES:])
        zero = jnp.zeros((8, LANES), jnp.float32)
        gp[j] = fold_rows(dots + [zero, zero])
        done_a = whole(buf_a, 15, sem_sa, sem_ra)
        done_a.wait_recv()
        nsum = buf_a[0, :, NBR : NBR + LANES]
        for s in range(1, NBLK):
            nsum = nsum + buf_a[s, :, NBR : NBR + LANES]
        nrow = jnp.sum(nsum, axis=0, keepdims=True)
        nsrc[...] = nrow
        for o in range(1, NGRP):
            pltpu.make_async_remote_copy(
                src_ref=nsrc, dst_ref=nbuf.at[slot, g], send_sem=sem_sn.at[slot], recv_sem=sem_rn.at[slot],
                device_id=peer(o), device_id_type=MESH).start()
        nbuf[slot, g] = nrow
        coupled = near_couple(buf_a)
        z = block_mul(dinv, u - coupled)
        done_a.wait_send()
        buf_b[i] = z
        spread(buf_b, sem_sb, sem_rb)
        done_b = whole(buf_b, 15, sem_sb, sem_rb)
        done_b.wait_recv()
        coupled = near_couple(buf_b)
        z = block_mul(dinv, u - coupled)
        done_b.wait_send()
        buf_c[i] = z
        def far_send(t, c):
            dg = lax.rem(g + 1 + t // 2, NGRP)
            first = pl.multiple_of(dg * NBLK + lax.rem(t, 2) * 8, 8)
            idx = req[pl.ds(first, 8), :]
            lo, hi = idx & 127, lax.shift_right_logical(idx, 7)
            out = jnp.zeros((8, LANES), jnp.float32)
            for b in range(8):
                for h in range(2):
                    table = jnp.broadcast_to(buf_c[i, b : b + 1, h * LANES : (h + 1) * LANES], (8, LANES))
                    out = jnp.where((hi == h) & (lane_group == b), lane_pick(table, lo), out)
            fsrc[pl.ds(first, 8), :] = out
            for d in range(8):
                pltpu.make_async_remote_copy(
                    src_ref=fsrc.at[pl.ds(first + d, 1)], dst_ref=fbuf.at[slot, pl.ds(me, 1)],
                    send_sem=sem_sf, recv_sem=sem_rf.at[slot],
                    device_id=(dg, lax.rem(t, 2) * 8 + d), device_id_type=MESH).start()
            return c

        spread(buf_c, sem_sc, sem_rc)
        lax.fori_loop(0, 14, far_send, 0)
        ss[j] = z
        base = [jac[0, a] * z for a in range(8)]
        done_c = whole(buf_c, 15, sem_sc, sem_rc)
        done_c.wait_recv()
        picked = near_pick(buf_c)
        acc = base
        for k in range(7):
            acc = add_slot(acc, 1 + k, joined(picked[2 * k], picked[2 * k + 1]))
        done_c.wait_send()
        done_f = pltpu.make_async_remote_copy(
            src_ref=fsrc.at[pl.ds(0, 112)], dst_ref=fbuf.at[slot, pl.ds(0, 112)], send_sem=sem_sf, recv_sem=sem_rf.at[slot],
            device_id=mate(1), device_id_type=MESH)
        done_f.wait_recv()
        for q in range(16):
            x = jnp.zeros((8, LANES), jnp.float32)
            for o in range(8):
                rowv = jnp.broadcast_to(fbuf[slot, 8 * q + o : 8 * q + o + 1, :], (8, LANES))
                x = jnp.where(lane_group == o, lane_pick(rowv, turn), x)
            fpk[q] = x
        fpk[2 * g] = picked[14]
        fpk[2 * g + 1] = picked[15]
        for k in range(8):
            got = []
            for h in range(2):
                lo, hi = far_place(2 * k + h)
                x = jnp.zeros((8, LANES), jnp.float32)
                for v in range(16):
                    x = jnp.where(hi == v, lane_pick(fpk[v], lo), x)
                got.append(x)
            acc = add_slot(acc, 8 + k, joined(*got))
        image = fold_rows(acc)
        done_f.wait_send()
        done_n = pltpu.make_async_remote_copy(
            src_ref=nbuf.at[slot, pl.ds(0, 7)], dst_ref=nbuf.at[slot, pl.ds(0, 7)], send_sem=sem_sn.at[slot], recv_sem=sem_rn.at[slot],
            device_id=mate(1), device_id_type=MESH)
        done_n.wait_recv()
        done_n.wait_send()
        total = nbuf[slot, 0]
        for s in range(1, NGRP):
            total = total + nbuf[slot, s]
        scale = lax.rsqrt(jnp.maximum(jnp.sum(total, axis=1, keepdims=True), 1e-12))
        sig[j] = jnp.broadcast_to(scale, (8, LANES))
        us[j + 1] = (image - u) * scale
        return carry

    lax.fori_loop(0, KRYLOV, step, 0)

    u = us[KRYLOV]
    dots = []
    for l in range(6):
        t = u * us[l]
        dots.append(t[:, :LANES] + t[:, LANES:])
    zero = jnp.zeros((8, LANES), jnp.float32)
    gp[KRYLOV] = fold_rows(dots + [zero, zero])
    row = jnp.zeros((1, LANES), jnp.float32)
    lane = iota((8, LANES), 1)
    sub = iota((8, LANES), 0)
    for j in range(6):
        s = jnp.sum(gp[j], axis=1, keepdims=True)
        row = row + jnp.sum(jnp.where(lane == 8 * j + sub, s, 0.0), axis=0, keepdims=True)
    rsrc[...] = row

    def tell(o, c):
        d = lax.rem(me + o, DEVICES)
        pltpu.make_async_remote_copy(
            src_ref=rsrc, dst_ref=rbuf.at[pl.ds(me, 1)], send_sem=sem_sf, recv_sem=sem_rf.at[2],
            device_id=(d // NBLK, lax.rem(d, NBLK)), device_id_type=MESH).start()
        return c

    lax.fori_loop(1, DEVICES, tell, 0)
    rbuf[pl.ds(me, 1), :] = row
    done = whole(rbuf, 127, sem_sf, sem_rf.at[2])
    done.wait_recv()
    done.wait_send()
    total = rbuf[0:8, :]
    for q in range(1, 16):
        total = total + rbuf[8 * q : 8 * q + 8, :]
    total = jnp.sum(total, axis=0, keepdims=True)
    gram = [[jnp.broadcast_to(total[:, 8 * j + l : 8 * j + l + 1], (8, LANES)) for l in range(j + 1)] for j in range(6)]
    weights = small_solve(gram, [sig[j] for j in range(KRYLOV)])
    for h in range(2):
        part = slice(h * LANES, (h + 1) * LANES)
        x = weights[0] * ss[0, :, part]
        for l in range(1, KRYLOV):
            x = x + weights[l] * ss[l, :, part]
        upd[:, part] = x
    pre[...] = ss[0]


def krylov(jacobian, inverse, newton_residual, block_cols):
    vm = pl.BlockSpec(memory_space=pltpu.VMEM)
    f32, i32 = jnp.float32, jnp.int32
    dma = pltpu.SemaphoreType.DMA
    return pl.pallas_call(
        krylov_kernel,
        out_shape=(jax.ShapeDtypeStruct((8, NBR), f32), jax.ShapeDtypeStruct((8, NBR), f32)),
        in_specs=[vm] * 4,
        out_specs=(vm, vm),
        scratch_shapes=[
            pltpu.VMEM((NBLK, 8, NBR + LANES), f32),
            pltpu.VMEM((NBLK, 8, NBR), f32),
            pltpu.VMEM((NBLK, 8, NBR), f32),
            pltpu.VMEM((DEVICES, LANES), f32),
            pltpu.VMEM((2, DEVICES, LANES), f32),
            pltpu.VMEM((DEVICES, LANES), i32),
            pltpu.VMEM((DEVICES, LANES), i32),
            pltpu.VMEM((1, LANES), f32),
            pltpu.VMEM((2, NGRP, 1, LANES), f32),
            pltpu.VMEM((1, LANES), f32),
            pltpu.VMEM((DEVICES, LANES), f32),
            pltpu.VMEM((KRYLOV + 1, 8, NBR), f32),
            pltpu.VMEM((KRYLOV, 8, NBR), f32),
            pltpu.VMEM((KRYLOV + 1, 8, LANES), f32),
            pltpu.VMEM((KRYLOV, 8, LANES), f32),
            pltpu.VMEM((8, NBR), i32),
            pltpu.VMEM((1, NBR), i32),
            pltpu.VMEM((16, 8, LANES), f32),
            dma, dma, dma, dma, dma((3,)), dma, dma, dma, dma((3,)), dma((3,)),
        ],
        compiler_params=pltpu.CompilerParams(collective_id=0, has_side_effects=True, vmem_limit_bytes=32 * 1024 * 1024),
    )(jacobian, inverse, newton_residual, block_cols)


GRP = ("grp",)
BLK = ("blk",)
GRP_BLK = ("grp", "blk")


def sent_together(arrays, axis, split_dim, concat_dim, along):
    columns = [a.reshape(*a.shape[:along], -1) for a in arrays]
    both = jnp.concatenate(columns, axis=along)
    result, at, done = (
        lax.all_to_all(both, axis, split_axis=split_dim, concat_axis=concat_dim, tiled=True),
        0,
        [],
    )
    for a, column in zip(arrays, columns):
        piece = result[..., at : at + column.shape[along]]
        done.append(piece.reshape(*piece.shape[:along], *a.shape[along:]))
        at += column.shape[along]
    return tuple(done)


def passed_along(block, axis, distance):
    devices = range(lax.axis_size(axis))
    route = [((i - distance) % len(devices), i) for i in devices]
    return lax.ppermute(block, axis, route)


def invert_blocks(diag):
    size = diag.shape[0]
    eye_mat = jnp.eye(size, dtype=jnp.float32)[:, :, None]
    inverse = eye_mat * jnp.ones_like(diag[:1])
    work = diag
    for pivot_row in range(size):
        scale = 1.0 / work[pivot_row, pivot_row]
        top_work = work[pivot_row] * scale
        top_inverse = inverse[pivot_row] * scale
        factor = work[:, pivot_row]
        work = work - factor[:, None, :] * top_work[None]
        inverse = inverse - factor[:, None, :] * top_inverse[None]
        work = work.at[pivot_row].set(top_work)
        inverse = inverse.at[pivot_row].set(top_inverse)
    return inverse


def add_stamps(summed, values, targets, counts, offset, local_rows):
    slots = values.shape[2]
    slot_ids = offset + jnp.arange(slots, dtype=jnp.int32)
    live = slot_ids[None, :] < counts
    masked = jnp.where(live[:, None, :], values, 0.0)
    index_pairs = jnp.stack([targets // local_rows, targets % local_rows], axis=2).astype(jnp.int32)
    numbers = lax.ScatterDimensionNumbers(
        update_window_dims=(1,), inserted_window_dims=(0, 2), scatter_dims_to_operand_dims=(0, 2)
    )
    return lax.scatter_add(summed, index_pairs, masked, numbers)


def local(stamps, stamp_target, pair_counts, conductance, block_cols, newton_residual):
    grp_count = lax.axis_size(GRP)
    blk_count = lax.axis_size(BLK)
    devices = grp_count * blk_count
    local_rows = conductance.shape[1]
    capacity = stamps.shape[3]
    summed = jnp.zeros((K, 64, local_rows), jnp.float32)
    front = capacity // 4
    got_values, got_target, got_counts = (
        lax.all_to_all(stamps[:, :, :, :front], GRP_BLK, split_axis=1, concat_axis=0, tiled=True),
        *sent_together((stamp_target[:, :, :front], pair_counts), GRP_BLK, 1, 0, 2),
    )
    summed = add_stamps(
        summed,
        got_values.reshape(devices, 64, front),
        got_target.reshape(devices, front),
        got_counts,
        0,
        local_rows,
    )
    my_index = lax.axis_index(GRP_BLK)
    next_index = (my_index + 1) % devices
    own_values = lax.dynamic_index_in_dim(stamps[0], my_index, 0, keepdims=False)[:, front:]
    own_target = lax.dynamic_index_in_dim(stamp_target[0], my_index, 0, keepdims=False)[front:]
    own_count = lax.dynamic_index_in_dim(pair_counts[0], my_index, 0, keepdims=True)
    next_values = lax.dynamic_index_in_dim(stamps[0], next_index, 0, keepdims=False)[:, front:]
    next_target = lax.dynamic_index_in_dim(stamp_target[0], next_index, 0, keepdims=False)[front:]
    next_count = lax.dynamic_index_in_dim(pair_counts[0], next_index, 0, keepdims=True)
    prior_values, prior_target, prior_count = passed_along(
        (next_values, next_target, next_count), GRP_BLK, 1
    )
    tail_values = jnp.stack([own_values, prior_values], axis=0)
    tail_target = jnp.stack([own_target, prior_target], axis=0)
    tail_counts = jnp.stack([own_count, prior_count], axis=0)
    summed = add_stamps(summed, tail_values, tail_target, tail_counts, front, local_rows)
    jacobian = summed.reshape(K, 8, 8, local_rows)
    identity = jnp.eye(8, dtype=jnp.float32)
    jacobian = jacobian.at[0].add(identity[:, :, None] * conductance[:, None, :])
    inverse = invert_blocks(jacobian[0])
    update, preconditioned = krylov(jacobian, inverse, newton_residual, block_cols)
    return update, jacobian, preconditioned


def solution(mesh):
    return jax.shard_map(
        local,
        mesh=mesh,
        in_specs=(
            P(GRP_BLK, None, None, None),
            P(GRP_BLK, None, None),
            P(GRP_BLK, None),
            P(None, GRP_BLK),
            P(None, GRP_BLK),
            P(None, GRP_BLK),
        ),
        out_specs=(P(None, GRP_BLK), P(None, None, None, GRP_BLK), P(None, GRP_BLK)),
        check_vma=False,
    )
```

time: 1040 us -> 221 us (0.21); the launches traced: 1030 us -> 221 us
  blocking collectives: 409 us -> 0 us
  local copies, waits for them, and re-layouts: 323 us -> 15 us
  Pallas kernels: 0 us -> 118 us
  waiting for transfers between devices: 134 us -> 17.9 us
  other arithmetic: 97.2 us -> 43.1 us
  between operations: 30.3 us -> 1.2 us
    gather x15 -> x0, local copies, waits for them, and re-layouts: 224 us -> none  [the longest x10 141 us: local(): precondition_picked = jnp.where(near[None], grouped[:, local_cols], 0.0)]
    psum x24 -> x0, blocking collectives: 196 us -> none  [by_axis(): array = lax.psum(array, axis)]
    all_gather x15 -> x0, blocking collectives: 146 us -> none  [all_blocks(): parts = lax.all_gather(parts, axes[k], axis=0, tiled=True)]
    pallas_call x0 -> x1, Pallas kernels: none -> 118 us  [krylov(): pl.pallas_call(krylov_kernel, out_shape=(jax.ShapeDtypeStruct((8, NBR), f...]
    all_gather x5 -> x0, waiting for transfers between devices: 97.8 us -> none  [all_blocks(): parts = lax.all_gather(parts, axes[k], axis=0, tiled=True)]
    all_to_all x7 -> x0, blocking collectives: 67.6 us -> none  [copy_for_each(): lax.all_to_all(jnp.broadcast_to(array[None], (length, *array.shape)), axi...]
    transpose x15 -> x0, local copies, waits for them, and re-layouts: 55 us -> none  [the longest x5 49.1 us: all_blocks(): parts.transpose(*turned, *range(len(sequence), parts.ndim))]
    unnamed x26 -> x4, other arithmetic: 42.9 us -> 23.5 us
  transfers between devices with their start and end apart: 13 -> 5, of which waited for: 9 -> 1; matrix products, arithmetic and copies ran while one was open for 3% -> 5% of each run, Pallas kernels for 0% -> 0%
where the time goes in v1:
time: 221 us
  Pallas kernels  118 us (53%)
  other arithmetic  43.1 us (20%)
  starting transfers between devices  25.1 us (11%)
  waiting for transfers between devices  17.9 us (8%)
  local copies, waits for them, and re-layouts  15 us (7%)
    pallas_call x1, Pallas kernels, krylov(): pl.pallas_call(krylov_kernel, out_shape=(jax.ShapeDtypeStruct((8, NBR), f...  118 us
    unnamed x4, other arithmetic  23.5 us
    all_to_all x1, waiting for transfers between devices, local(): lax.all_to_all(stamps[:, :, :, :front], GRP_BLK, split_axis=1, concat_axi...  17.9 us
    all_to_all x1, starting transfers between devices, sent_together(): lax.all_to_all(both, axis, split_axis=split_dim, concat_axis=concat_dim,...  11.5 us
    scatter-add x1, other arithmetic, add_stamps(): return lax.scatter_add(summed, index_pairs, masked, numbers)  9.91 us
    all_to_all x1, starting transfers between devices, local(): lax.all_to_all(stamps[:, :, :, :front], GRP_BLK, split_axis=1, concat_axi...  9.51 us
    unnamed x28, local copies, waits for them, and re-layouts  9.41 us
  transfers between devices with their start and end apart: 5, of which 1 were waited for; matrix products, arithmetic and copies ran while one was open for 5% of the time, Pallas kernels for 0%

profile of v1, /device:TPU:1, one launch (start us, length us, event | category | flops | bytes accessed | tf_op | source)
XLA Modules:
  0.0 220.9 jit_solution(18262683663660590119)
XLA Ops:
  0.6 0.9 copy.57
  1.5 0.7 pad_add_fusion.1
  2.2 0.7 copy.37
  2.9 11.5 %all-to-all-start = ((s32[1,128,33]{2,0,1:T(1,128)}), s32[1,128,33]{2,0,1:T(1,128)S(1)}, u32[]{:S(2)}, u32[]{:S(2)}) async-start(s32[1,128,33]{2,0,1:T(1,128)} %copy.37), calls=%async_computation | async-start | bytes 131072 | tf_op jit(solution)/shard_map/all_to_all | solution.py:447
  14.5 0.8 constant_dynamic-slice_fusion.3
  15.3 1.5 collective-permute-start
  16.8 0.8 dynamic-slice_bitcast_fusion.1
  17.7 1.5 collective-permute-start.2
  19.1 1.3 constant_dynamic-slice_fusion.1
  20.4 1.2 collective-permute-start.1
  21.6 2.8 %copy.58 = f32[1,128,64,32]{2,3,0,1:T(8,128)S(1)} copy(f32[1,128,64,32]{3,2,1,0:T(8,128)} %bitcast.130) | data formatting | bytes 2097152
  24.5 2.3 %reshape.1221 = f32[128,1,2048]{2,1,0:T(1,128)} reshape(f32[128,1,32,64]{3,2,1,0:T(8,128)S(1)} %bitcast.129) | data formatting | bytes 2097152
  26.9 1.3 add_reduce_fusion
  28.4 9.5 %all-to-all-start.1 = ((f32[128,1,2048]{2,1,0:T(1,128)}), f32[128,1,2048]{2,1,0:T(1,128)S(1)}, u32[]{:S(2)}, u32[]{:S(2)}) async-start(f32[128,1,2048]{2,1,0:T(1,128)} %reshape.1221), calls=%async_computation.1 | async-start | bytes 2097152 | tf_op jit(solution)/shard_map/all_to_all | solution.py:502
  38.9 17.9 %all-to-all-done.1 = f32[128,1,2048]{2,1,0:T(1,128)S(1)} async-done(((f32[128,1,2048]{2,1,0:T(1,128)}), f32[128,1,2048]{2,1,0:T(1,128)S(1)}, u32[]{:S(2)}, u32[]{:S(2)}) %all-to-all-start.1) | async-done | bytes 1048608 | tf_op jit(solution)/shard_map/all_to_all | solution.py:502
  57.4 4.3 %reduce.44 = f32[128,2048]{1,0:T(8,128)} reduce(f32[128,1,2048]{2,1,0:T(1,128)S(1)} %all-to-all-done.1, f32[]{:T(128)} %broadcast.716), dimensions={1}, to_apply=%all_to_all.8.reduce_sub_computation | reduce | bytes 2097156 | tf_op jit(solution)/shard_map/all_to_all | solution.py:502
  61.7 2.0 reshape.1222
  63.7 2.4 %bitcast_select_fusion = f32[128,64,32]{1,2,0:T(8,128)} fusion(pred[128,32]{1,0:T(8,128)(4,1)S(1)} %iota_compare_fusion, f32[128,1,32,64]{3,2,1,0:T(8,128)S(1)} %reshape.1222), kind=kLoop, calls=%fused_computation.2 | loop fusion | flops 262144 | bytes 2101248 | tf_op jit(solution)/shard_map/jit(_where)/select_n | solution.py:485
  66.1 23.3 %scatter_custom_fusion.1 = f32[4096,64]{1,0:T(8,128)S(1)} fusion(s32[4096]{0:T(1024)S(1)} %reshape.1204, f32[4096,64]{1,0:T(8,128)} %bitcast.131, f32[]{:T(128)} %constant.465.clone.1), kind=kCustom, calls=%fused_computation.3 | custom fusion | flops 262144 | bytes 1049088
  89.5 9.9 %scatter_fusion = f32[16,64,256]{1,2,0:T(8,128)S(1)} fusion(f32[16,64,256]{1,2,0:T(8,128)S(1)} %bitcast.128, s32[192]{0:T(256)S(1)} %reshape.1198, f32[192,64]{1,0:T(8,128)S(1)} %bitcast.135), kind=kCustom, calls=%fused_computation | custom fusion | flops 12288 | bytes 148992 | tf_op jit(solution)/shard_map/scatter-add | solution.py:490
  99.4 0.6 copy.44
  101.2 118.5 %shard_map.85 = (f32[8,256]{1,0:T(8,128)S(1)}, f32[8,256]{1,0:T(8,128)S(1)}) custom-call(f32[16,8,8,256]{3,2,1,0:T(8,128)S(1)} %get-tuple-element.255.jac, f32[8,8,256]{2,1,0:T(8,128)S(1)} %fusion.31.dinv, f32[8,256]{1,0:T(8,128)S(1)} %copy-done.2, s32[16,256]{1,0:T(8,128)S(1)} %copy-done.1), custom_call_target="tpu_custom_call" | custom-call | tf_op jit(solution)/shard_map/pallas_call | solution.py:408
  219.7 0.6 copy.94
  220.3 0.6 copy.95
  (92 shorter events, 2.8 us)
Async XLA Ops:
  2.9 25.5 %all-to-all-start = ((s32[1,128,33]{2,0,1:T(1,128)}), s32[1,128,33]{2,0,1:T(1,128)S(1)}, u32[]{:S(2)}, u32[]{:S(2)}) async-start(s32[1,128,33]{2,0,1:T(1,128)} %copy.37), calls=%async_computation | async-start | bytes 131072 | tf_op jit(solution)/shard_map/all_to_all | solution.py:447
  15.3 13.0 %collective-permute-start = (s32[96]{0:T(128)S(1)}, s32[96]{0:T(128)S(1)}, u32[]{:S(2)}, u32[]{:S(2)}) collective-permute-start(s32[96]{0:T(128)S(1)} %slice_bitcast_fusion.2), channel_id=1, source_target_pairs={{127,0},{0,1},{1,2},{2,3},{3,4},{4,5},{5,6},{6,7},{7,8},{8,9},{9,1... | collective-permute-start | bytes 1160 | tf_op jit(solution)/shard_map/ppermute | solution.py:461
  17.7 21.1 %collective-permute-start.2 = (f32[64,96]{1,0:T(8,128)S(1)}, f32[64,96]{1,0:T(8,128)S(1)}, u32[]{:S(2)}, u32[]{:S(2)}) collective-permute-start(f32[64,96]{1,0:T(8,128)S(1)} %slice.504), channel_id=1, source_target_pairs={{127,0},{0,1},{1,2},{2,3},{3,4},{4,5},{5,6},{6,7},{7,8},{8,9},{9,1... | collective-permute-start | bytes 73736 | tf_op jit(solution)/shard_map/ppermute | solution.py:461
  20.4 6.4 %collective-permute-start.1 = (s32[1]{0:T(128)}, s32[1]{0:T(128)}, u32[]{:S(2)}, u32[]{:S(2)}) collective-permute-start(s32[1]{0:T(128)} %bitcast.11), channel_id=1, source_target_pairs={{127,0},{0,1},{1,2},{2,3},{3,4},{4,5},{5,6},{6,7},{7,8},{8,9},{9,1... | collective-permute-start | bytes 20 | tf_op jit(solution)/shard_map/ppermute | solution.py:461
  26.7 11.4 %copy-start.5 = (s32[2]{0:T(128)S(1)}, s32[2]{0:T(128)}, u32[]{:S(2)}) copy-start(s32[2]{0:T(128)} %constant.489) | copy-start | bytes 28
  26.7 11.5 %copy-start.4 = (s32[2]{0:T(128)S(1)}, s32[2]{0:T(128)}, u32[]{:S(2)}) copy-start(s32[2]{0:T(128)} %constant.492) | copy-start | bytes 28
  28.4 28.4 %all-to-all-start.1 = ((f32[128,1,2048]{2,1,0:T(1,128)}), f32[128,1,2048]{2,1,0:T(1,128)S(1)}, u32[]{:S(2)}, u32[]{:S(2)}) async-start(f32[128,1,2048]{2,1,0:T(1,128)} %reshape.1221), calls=%async_computation.1 | async-start | bytes 2097152 | tf_op jit(solution)/shard_map/all_to_all | solution.py:502
  99.4 0.7 copy-start.3
  100.0 1.2 copy-start.1
  100.0 1.2 copy-start.2
  100.3 120.6 %copy-start = (f32[16,8,8,256]{3,2,1,0:T(8,128)}, f32[16,8,8,256]{3,2,1,0:T(8,128)S(1)}, u32[]{:S(2)}) copy-start(f32[16,8,8,256]{3,2,1,0:T(8,128)S(1)} %get-tuple-element.255.jac) | copy-start | bytes 3145732

commit v2 on v1

--- a/solution.py
+++ b/solution.py
@@ -13,6 +13,7 @@
 NBLK = 16
 DEVICES = 128
 LANES = 128
+FRONT = 32
 EPS = 1e-06
 MESH = pl.DeviceIdType.MESH
 AXES = ("grp", "blk")
@@ -125,7 +126,8 @@
     return out
 
 
-def krylov_kernel(jac, dinv, res, cols, upd, pre,
+def solver_kernel(stamps, target, counts, cond, res, cols, upd, jac_out, pre,
+                  stage, sbuf, rbuf_s, trep, cntb, tail, ttail, ttsrc, jac, dinv, sem_h, sem_ss, sem_rs, sem_t, sem_j,
                   buf_a, buf_b, buf_c, fsrc, fbuf, req_src, req, nsrc, nbuf, rsrc, rbuf,
                   us, ss, gp, sig, pidx, lst, fpk,
                   sem_sa, sem_sb, sem_sc, sem_sf, sem_sn, sem_ra, sem_rb, sem_rc, sem_rf, sem_rn):
@@ -149,6 +151,69 @@
         return c
 
     lax.fori_loop(1, DEVICES, greet, 0)
+
+    my_chunk = me // 8
+
+    def load(t):
+        first = pl.multiple_of(lax.rem(my_chunk + t, 16) * 8, 8)
+        return pltpu.make_async_copy(stamps.at[0, pl.ds(first, 8)], stage.at[pl.ds(first, 8)], sem_h.at[t])
+
+    def start_load(t, c):
+        load(t).start()
+        return c
+
+    lax.fori_loop(0, 16, start_load, 0)
+    lane_big = iota((DEVICES, LANES), 1)
+    row_big = iota((DEVICES, LANES), 0)
+    count = jnp.sum(jnp.where(lane_big == row_big, counts[...], 0), axis=1, keepdims=True)
+    count = jnp.broadcast_to(count, (DEVICES, LANES))
+    cntb[...] = count
+    tgt = jnp.where((lane_big < count) & (row_big != me), target[...], -1)
+    trep[...] = lane_pick(tgt, lane_big & (FRONT - 1)).astype(jnp.float32)
+    nxt = lax.rem(me + 1, DEVICES)
+    lane1 = iota((1, LANES), 1)
+    ttsrc[...] = jnp.where((lane1 >= FRONT) & (lane1 < cntb[pl.ds(nxt, 1), :]), target[pl.ds(nxt, 1), :], -1).astype(jnp.float32)
+    own_target = jnp.where(lane1 < cntb[pl.ds(me, 1), :], target[pl.ds(me, 1), :], -1)
+    quarter = lax.shift_right_logical(iota((16, LANES), 1), 5)
+
+    def pack(first):
+        rows = trep[pl.ds(first, 8), :]
+        for e in range(8):
+            x = stage[first + e, 0:16, :]
+            for q in range(1, 4):
+                x = jnp.where(quarter == q, pltpu.roll(stage[first + e, 16 * q : 16 * q + 16, :], 32 * q, 1), x)
+            sbuf[first + e, 0:16, :] = x
+            sbuf[first + e, 16:17, :] = rows[e : e + 1]
+
+    def stamp_copy(d):
+        return pltpu.make_async_remote_copy(
+            src_ref=sbuf.at[d, pl.ds(0, 17)], dst_ref=rbuf_s.at[me, pl.ds(0, 17)], send_sem=sem_ss, recv_sem=sem_rs.at[my_chunk],
+            device_id=(d // NBLK, lax.rem(d, NBLK)), device_id_type=MESH)
+
+    load(0).wait()
+    own_first = pl.multiple_of(my_chunk * 8, 8)
+    pack(own_first)
+    rbuf_s[me] = sbuf[me]
+    pl.semaphore_wait(barrier, DEVICES - 1)
+    for e in range(1, 8):
+        stamp_copy(own_first + lax.rem(me + e, 8)).start()
+
+    def send_chunk(t, c):
+        load(t).wait()
+        first = pl.multiple_of(lax.rem(my_chunk + t, 16) * 8, 8)
+        pack(first)
+        for e in range(8):
+            stamp_copy(first + lax.rem(me + e, 8)).start()
+        return c
+
+    lax.fori_loop(1, 16, send_chunk, 0)
+    tail_dev = (nxt // NBLK, lax.rem(nxt, NBLK))
+    tail_copy = pltpu.make_async_remote_copy(
+        src_ref=stage.at[nxt], dst_ref=tail, send_sem=sem_t.at[0], recv_sem=sem_t.at[1], device_id=tail_dev, device_id_type=MESH)
+    tail_copy.start()
+    ttail_copy = pltpu.make_async_remote_copy(
+        src_ref=ttsrc, dst_ref=ttail, send_sem=sem_t.at[2], recv_sem=sem_t.at[3], device_id=tail_dev, device_id_type=MESH)
+    ttail_copy.start()
 
     owner_row = iota((DEVICES, NBR), 0)
     upper = bf(iota((NBR, NBR), 0) < iota((NBR, NBR), 1))
@@ -176,8 +241,6 @@
     req_src[...] = wanted.astype(jnp.int32)
     lst[...] = (lax.shift_right_logical(iota((8, NBR), 1), 4) * NBR + listed.astype(jnp.int32))[0:1]
 
-    pl.semaphore_wait(barrier, DEVICES - 1)
-
     def ask(t, c):
         dg, di = far_dev(t)
         d = dg * NBLK + di
@@ -196,6 +259,84 @@
             src_ref=ref.at[pl.ds(0, rows)], dst_ref=ref.at[pl.ds(0, rows)], send_sem=send, recv_sem=recv,
             device_id=mate(1), device_id_type=MESH)
 
+    jac[...] = jnp.zeros_like(jac)
+    node = iota((NBR, NBR), 0)
+
+    def add_slots(values, goal):
+        slot_k = lax.shift_right_arithmetic(goal, 8)
+        values = jnp.where(goal >= 0, values, 0.0)
+        high = values.astype(jnp.bfloat16)
+        low = (values - high.astype(jnp.float32)).astype(jnp.bfloat16)
+        both = jnp.concatenate([high, low], axis=1)
+        there = bf(node == (goal & 255))
+        there = jnp.concatenate([there, there], axis=1)
+        twice = jnp.concatenate([slot_k, slot_k], axis=1)
+        for k0 in range(0, K, 4):
+            rows = [both * bf(jnp.broadcast_to(twice == k0 + k, (64, 2 * NBR))) for k in range(4)]
+            part = lax.dot_general(jnp.concatenate(rows, axis=0), there, nt, preferred_element_type=jnp.float32)
+            jac[k0 : k0 + 4] = jac[k0 : k0 + 4] + part.reshape(4, 8, 8, NBR)
+
+    def add_chunk(first):
+        wide, goals = [], []
+        for tile in range(2):
+            blocks = [rbuf_s[first + 4 * tile + s, 0:16, :] for s in range(4)]
+            parts = []
+            for q in range(4):
+                x = None
+                for s in range(4):
+                    y = blocks[s] if s == q else pltpu.roll(blocks[s], (s - q) * 32 % LANES, 1)
+                    x = y if x is None else jnp.where(quarter == s, y, x)
+                parts.append(x)
+            wide.append(jnp.concatenate(parts, axis=0))
+            x = rbuf_s[first + 4 * tile, 16:17, :]
+            for s in range(1, 4):
+                x = jnp.where(quarter[0:1] == s, rbuf_s[first + 4 * tile + s, 16:17, :], x)
+            goals.append(x.astype(jnp.int32))
+        add_slots(jnp.concatenate(wide, axis=1), jnp.concatenate(goals, axis=1))
+
+    def chunk_wait(first, count, sem):
+        return pltpu.make_async_remote_copy(
+            src_ref=sbuf.at[pl.ds(0, count), pl.ds(0, 17)], dst_ref=rbuf_s.at[pl.ds(0, count), pl.ds(0, 17)],
+            send_sem=sem_ss, recv_sem=sem, device_id=mate(1), device_id_type=MESH)
+
+    chunk_wait(own_first, 7, sem_rs.at[my_chunk]).wait_recv()
+    add_chunk(own_first)
+
+    def take_chunk(t, c):
+        chunk = lax.rem(my_chunk + 16 - t, 16)
+        first = pl.multiple_of(chunk * 8, 8)
+        chunk_wait(first, 8, sem_rs.at[chunk]).wait_recv()
+        add_chunk(first)
+        return c
+
+    lax.fori_loop(1, 16, take_chunk, 0)
+    tail_copy.wait_recv()
+    ttail_copy.wait_recv()
+    add_slots(
+        jnp.concatenate([stage[me], tail[...]], axis=1),
+        jnp.concatenate([own_target, ttail[...].astype(jnp.int32)], axis=1))
+    sub8 = iota((8, NBR), 0)
+    for a in range(8):
+        jac[0, a] = jac[0, a] + jnp.where(sub8 == a, jnp.broadcast_to(cond[a : a + 1, :], (8, NBR)), 0.0)
+    jac_copy = pltpu.make_async_copy(jac, jac_out, sem_j)
+    jac_copy.start()
+
+    work = [jac[0, a] for a in range(8)]
+    inverse = [jnp.where(sub8 == a, 1.0, 0.0) for a in range(8)]
+    for p in range(8):
+        scale = 1.0 / work[p][p : p + 1, :]
+        top_w, top_i = work[p] * scale, inverse[p] * scale
+        for a in range(8):
+            if a != p:
+                factor = work[a][p : p + 1, :]
+                work[a] = work[a] - factor * top_w
+                inverse[a] = inverse[a] - factor * top_i
+        work[p], inverse[p] = top_w, top_i
+    for a in range(8):
+        dinv[a] = inverse[a]
+    chunk_wait(own_first, 127, sem_ss).wait_send()
+    tail_copy.wait_send()
+    ttail_copy.wait_send()
     asked = whole(req, 112, sem_sn.at[2], sem_rn.at[2])
     asked.wait_recv()
     asked.wait_send()
@@ -399,18 +540,35 @@
             x = x + weights[l] * ss[l, :, part]
         upd[:, part] = x
     pre[...] = ss[0]
-
-
-def krylov(jacobian, inverse, newton_residual, block_cols):
+    jac_copy.wait()
+
+
+def local(stamps, stamp_target, pair_counts, conductance, block_cols, newton_residual):
     vm = pl.BlockSpec(memory_space=pltpu.VMEM)
+    hbm = pl.BlockSpec(memory_space=pl.ANY)
     f32, i32 = jnp.float32, jnp.int32
     dma = pltpu.SemaphoreType.DMA
     return pl.pallas_call(
-        krylov_kernel,
-        out_shape=(jax.ShapeDtypeStruct((8, NBR), f32), jax.ShapeDtypeStruct((8, NBR), f32)),
-        in_specs=[vm] * 4,
-        out_specs=(vm, vm),
+        solver_kernel,
+        out_shape=(
+            jax.ShapeDtypeStruct((8, NBR), f32),
+            jax.ShapeDtypeStruct((K, 8, 8, NBR), f32),
+            jax.ShapeDtypeStruct((8, NBR), f32),
+        ),
+        in_specs=[hbm] + [vm] * 5,
+        out_specs=(vm, hbm, vm),
         scratch_shapes=[
+            pltpu.VMEM((DEVICES, 64, LANES), f32),
+            pltpu.VMEM((DEVICES, 24, LANES), f32),
+            pltpu.VMEM((DEVICES, 24, LANES), f32),
+            pltpu.VMEM((DEVICES, LANES), f32),
+            pltpu.VMEM((DEVICES, LANES), i32),
+            pltpu.VMEM((64, LANES), f32),
+            pltpu.VMEM((1, LANES), f32),
+            pltpu.VMEM((1, LANES), f32),
+            pltpu.VMEM((K, 8, 8, NBR), f32),
+            pltpu.VMEM((8, 8, NBR), f32),
+            dma((16,)), dma, dma((16,)), dma((4,)), dma,
             pltpu.VMEM((NBLK, 8, NBR + LANES), f32),
             pltpu.VMEM((NBLK, 8, NBR), f32),
             pltpu.VMEM((NBLK, 8, NBR), f32),
@@ -431,106 +589,8 @@
             pltpu.VMEM((16, 8, LANES), f32),
             dma, dma, dma, dma, dma((3,)), dma, dma, dma, dma((3,)), dma((3,)),
         ],
-        compiler_params=pltpu.CompilerParams(collective_id=0, has_side_effects=True, vmem_limit_bytes=32 * 1024 * 1024),
-    )(jacobian, inverse, newton_residual, block_cols)
-
-
-GRP = ("grp",)
-BLK = ("blk",)
-GRP_BLK = ("grp", "blk")
-
-
-def sent_together(arrays, axis, split_dim, concat_dim, along):
-    columns = [a.reshape(*a.shape[:along], -1) for a in arrays]
-    both = jnp.concatenate(columns, axis=along)
-    result, at, done = (
-        lax.all_to_all(both, axis, split_axis=split_dim, concat_axis=concat_dim, tiled=True),
-        0,
-        [],
-    )
-    for a, column in zip(arrays, columns):
-        piece = result[..., at : at + column.shape[along]]
-        done.append(piece.reshape(*piece.shape[:along], *a.shape[along:]))
-        at += column.shape[along]
-    return tuple(done)
-
-
-def passed_along(block, axis, distance):
-    devices = range(lax.axis_size(axis))
-    route = [((i - distance) % len(devices), i) for i in devices]
-    return lax.ppermute(block, axis, route)
-
-
-def invert_blocks(diag):
-    size = diag.shape[0]
-    eye_mat = jnp.eye(size, dtype=jnp.float32)[:, :, None]
-    inverse = eye_mat * jnp.ones_like(diag[:1])
-    work = diag
-    for pivot_row in range(size):
-        scale = 1.0 / work[pivot_row, pivot_row]
-        top_work = work[pivot_row] * scale
-        top_inverse = inverse[pivot_row] * scale
-        factor = work[:, pivot_row]
-        work = work - factor[:, None, :] * top_work[None]
-        inverse = inverse - factor[:, None, :] * top_inverse[None]
-        work = work.at[pivot_row].set(top_work)
-        inverse = inverse.at[pivot_row].set(top_inverse)
-    return inverse
-
-
-def add_stamps(summed, values, targets, counts, offset, local_rows):
-    slots = values.shape[2]
-    slot_ids = offset + jnp.arange(slots, dtype=jnp.int32)
-    live = slot_ids[None, :] < counts
-    masked = jnp.where(live[:, None, :], values, 0.0)
-    index_pairs = jnp.stack([targets // local_rows, targets % local_rows], axis=2).astype(jnp.int32)
-    numbers = lax.ScatterDimensionNumbers(
-        update_window_dims=(1,), inserted_window_dims=(0, 2), scatter_dims_to_operand_dims=(0, 2)
-    )
-    return lax.scatter_add(summed, index_pairs, masked, numbers)
-
-
-def local(stamps, stamp_target, pair_counts, conductance, block_cols, newton_residual):
-    grp_count = lax.axis_size(GRP)
-    blk_count = lax.axis_size(BLK)
-    devices = grp_count * blk_count
-    local_rows = conductance.shape[1]
-    capacity = stamps.shape[3]
-    summed = jnp.zeros((K, 64, local_rows), jnp.float32)
-    front = capacity // 4
-    got_values, got_target, got_counts = (
-        lax.all_to_all(stamps[:, :, :, :front], GRP_BLK, split_axis=1, concat_axis=0, tiled=True),
-        *sent_together((stamp_target[:, :, :front], pair_counts), GRP_BLK, 1, 0, 2),
-    )
-    summed = add_stamps(
-        summed,
-        got_values.reshape(devices, 64, front),
-        got_target.reshape(devices, front),
-        got_counts,
-        0,
-        local_rows,
-    )
-    my_index = lax.axis_index(GRP_BLK)
-    next_index = (my_index + 1) % devices
-    own_values = lax.dynamic_index_in_dim(stamps[0], my_index, 0, keepdims=False)[:, front:]
-    own_target = lax.dynamic_index_in_dim(stamp_target[0], my_index, 0, keepdims=False)[front:]
-    own_count = lax.dynamic_index_in_dim(pair_counts[0], my_index, 0, keepdims=True)
-    next_values = lax.dynamic_index_in_dim(stamps[0], next_index, 0, keepdims=False)[:, front:]
-    next_target = lax.dynamic_index_in_dim(stamp_target[0], next_index, 0, keepdims=False)[front:]
-    next_count = lax.dynamic_index_in_dim(pair_counts[0], next_index, 0, keepdims=True)
-    prior_values, prior_target, prior_count = passed_along(
-        (next_values, next_target, next_count), GRP_BLK, 1
-    )
-    tail_values = jnp.stack([own_values, prior_values], axis=0)
-    tail_target = jnp.stack([own_target, prior_target], axis=0)
-    tail_counts = jnp.stack([own_count, prior_count], axis=0)
-    summed = add_stamps(summed, tail_values, tail_target, tail_counts, front, local_rows)
-    jacobian = summed.reshape(K, 8, 8, local_rows)
-    identity = jnp.eye(8, dtype=jnp.float32)
-    jacobian = jacobian.at[0].add(identity[:, :, None] * conductance[:, None, :])
-    inverse = invert_blocks(jacobian[0])
-    update, preconditioned = krylov(jacobian, inverse, newton_residual, block_cols)
-    return update, jacobian, preconditioned
+        compiler_params=pltpu.CompilerParams(collective_id=0, has_side_effects=True, vmem_limit_bytes=48 * 1024 * 1024),
+    )(stamps, stamp_target.reshape(DEVICES, LANES), pair_counts, conductance, newton_residual, block_cols)
 
 
 def solution(mesh):
@@ -538,13 +598,13 @@
         local,
         mesh=mesh,
         in_specs=(
-            P(GRP_BLK, None, None, None),
-            P(GRP_BLK, None, None),
-            P(GRP_BLK, None),
-            P(None, GRP_BLK),
-            P(None, GRP_BLK),
-            P(None, GRP_BLK),
+            P(AXES, None, None, None),
+            P(AXES, None, None),
+            P(AXES, None),
+            P(None, AXES),
+            P(None, AXES),
+            P(None, AXES),
         ),
-        out_specs=(P(None, GRP_BLK), P(None, None, None, GRP_BLK), P(None, GRP_BLK)),
+        out_specs=(P(None, AXES), P(None, None, None, AXES), P(None, AXES)),
         check_vma=False,
     )

time: 221 us -> 145 us (0.66)
  other arithmetic: 43.1 us -> 0 us
  starting transfers between devices: 25.1 us -> 0 us
  Pallas kernels: 118 us -> 136 us
  waiting for transfers between devices: 17.9 us -> 0 us
  local copies, waits for them, and re-layouts: 15 us -> 7.95 us
    unnamed x4 -> x0, other arithmetic: 23.5 us -> none
    all_to_all x2 -> x0, starting transfers between devices: 21 us -> none  [the longest x1 11.5 us: sent_together(): lax.all_to_all(both, axis, split_axis=split_dim, concat_axis=concat_dim,...]
    pallas_call x1, Pallas kernels: 118 us -> 136 us  [local(): pl.pallas_call(solver_kernel, out_shape=(jax.ShapeDtypeStruct((8, NBR), f...]
    all_to_all x2 -> x0, waiting for transfers between devices: 17.9 us -> none  [the longest x1 17.9 us: local(): lax.all_to_all(stamps[:, :, :, :front], GRP_BLK, split_axis=1, concat_axi...]
    scatter-add x2 -> x0, other arithmetic: 9.99 us -> none  [the longest x1 9.91 us: add_stamps(): return lax.scatter_add(summed, index_pairs, masked, numbers)]
    all_to_all x1 -> x0, other arithmetic: 4.33 us -> none  [local(): lax.all_to_all(stamps[:, :, :, :front], GRP_BLK, split_axis=1, concat_axi...]
    ppermute x3 -> x0, starting transfers between devices: 4.13 us -> none  [passed_along(): return lax.ppermute(block, axis, route)]
    select_n x4 -> x0, other arithmetic: 2.52 us -> none  [the longest x2 2.44 us: add_stamps(): masked = jnp.where(live[:, None, :], values, 0.0)]
  transfers between devices with their start and end apart: 5 -> 0, of which waited for: 1 -> 0; matrix products, arithmetic and copies ran while one was open for 5% -> 0% of each run, Pallas kernels for 0% -> 0%
where the time goes in v2:
time: 145 us
  Pallas kernels  136 us (94%)
  local copies, waits for them, and re-layouts  7.95 us (5%)
    pallas_call x1, Pallas kernels, local(): pl.pallas_call(solver_kernel, out_shape=(jax.ShapeDtypeStruct((8, NBR), f...  136 us
    unnamed x15, local copies, waits for them, and re-layouts  7.95 us

profile of v2, /device:TPU:1, one launch (start us, length us, event | category | flops | bytes accessed | tf_op | source)
XLA Modules:
  0.0 145.1 jit_solution(12741412996111686988)
XLA Ops:
  0.6 0.0 copy-start
  0.6 2.2 %copy-done = f32[1,128,64,128]{3,2,1,0:T(8,128)S(1)} copy-done((f32[1,128,64,128]{3,2,1,0:T(8,128)S(1)}, f32[1,128,64,128]{3,2,1,0:T(8,128)}, u32[]{:S(2)}) %copy-start) | copy-done | bytes 4194328
  2.8 0.0 copy-start.1
  2.8 0.8 copy-done.1
  3.7 0.0 copy-start.2
  3.7 0.7 copy-done.2
  4.4 0.0 copy-start.3
  4.4 0.7 copy-done.3
  5.1 0.0 copy-start.4
  5.1 0.7 copy-done.4
  5.8 0.0 copy-start.5
  5.8 0.7 copy-done.5
  6.4 136.4 %shard_map.85 = (f32[8,256]{1,0:T(8,128)S(1)}, f32[16,8,8,256]{3,2,1,0:T(8,128)S(1)}, f32[8,256]{1,0:T(8,128)S(1)}) custom-call(f32[1,128,64,128]{3,2,1,0:T(8,128)S(1)} %copy-done, s32[128,128]{1,0:T(8,128)S(1)} %bitcast.1, s32[1,128]{1,0:T(1,128)S(1)} %copy-done.5, f32[8,256]{1,0:T(8,128)S(1)} %copy-done.3, f32[8,256]{1,0:T(8,128)S(1)} %copy-done.4, ...), custom_call_target="tpu_custom_call" | custom-call | tf_op jit(solution)/shard_map/pallas_call | solution.py:551
  142.9 0.6 copy.12
  143.5 1.0 copy.13
  144.5 0.6 copy.14
Async XLA Ops:
  0.6 2.2 %copy-start = (f32[1,128,64,128]{3,2,1,0:T(8,128)S(1)}, f32[1,128,64,128]{3,2,1,0:T(8,128)}, u32[]{:S(2)}) copy-start(f32[1,128,64,128]{3,2,1,0:T(8,128)} %stamps.1) | copy-start | bytes 12582916
  2.8 0.8 copy-start.1
  3.7 0.7 copy-start.2
  4.4 0.7 copy-start.3
  5.1 0.7 copy-start.4
  5.8 0.7 copy-start.5

commit v3 on v2

--- a/solution.py
+++ b/solution.py
@@ -126,94 +126,64 @@
     return out
 
 
-def solver_kernel(stamps, target, counts, cond, res, cols, upd, jac_out, pre,
+def solver_kernel(stamps, target_in, counts_in, cond_in, res_in, cols_in, upd_out, jac_out, pre_out,
+                  target, counts, cond, res, cols, upd, idx_lo, idx_hi, far_lo, far_hi, sem_i, sem_o,
                   stage, sbuf, rbuf_s, trep, cntb, tail, ttail, ttsrc, jac, dinv, sem_h, sem_ss, sem_rs, sem_t, sem_j,
                   buf_a, buf_b, buf_c, fsrc, fbuf, req_src, req, nsrc, nbuf, rsrc, rbuf,
-                  us, ss, gp, sig, pidx, lst, fpk,
+                  us, ss, gp, sig, pidx, lst,
                   sem_sa, sem_sb, sem_sc, sem_sf, sem_sn, sem_ra, sem_rb, sem_rc, sem_rf, sem_rn):
     g, i = lax.axis_index("grp"), lax.axis_index("blk")
     me = g * NBLK + i
 
     def mate(o):
-        return (g, lax.rem(i + o, NBLK))
+        return (g, (i + o) & (NBLK - 1))
 
     def peer(o):
-        return (lax.rem(g + o, NGRP), i)
+        return ((g + o) & (NGRP - 1), i)
 
     def far_dev(t):
-        return lax.rem(g + 1 + t // NBLK, NGRP), lax.rem(i + t, NBLK)
+        return (g + 1 + t // NBLK) & (NGRP - 1), (i + t) & (NBLK - 1)
 
     barrier = pltpu.get_barrier_semaphore()
 
-    def greet(o, c):
-        d = lax.rem(me + o, DEVICES)
-        pl.semaphore_signal(barrier, inc=1, device_id=(d // NBLK, lax.rem(d, NBLK)), device_id_type=MESH)
+    def farthest_first(t):
+        low = t & 37
+        return me ^ (((low ^ 37) << 1) | (low ^ ((t >> 1) & 37)) | (~t & 16))
+
+    def chunk_at(t):
+        low = (t >> 2) & 1
+        return my_chunk ^ (((low ^ 1) << 3) | ((low ^ (t >> 3)) << 2) | (~t & 3))
+
+    def greet(t, c):
+        d = farthest_first(t)
+        pl.semaphore_signal(barrier, inc=1, device_id=(d // NBLK, d & (NBLK - 1)), device_id_type=MESH)
         return c
 
-    lax.fori_loop(1, DEVICES, greet, 0)
+    lax.fori_loop(0, DEVICES - 1, greet, 0)
 
     my_chunk = me // 8
 
     def load(t):
-        first = pl.multiple_of(lax.rem(my_chunk + t, 16) * 8, 8)
+        first = pl.multiple_of(((my_chunk + t) & 15) * 8, 8)
         return pltpu.make_async_copy(stamps.at[0, pl.ds(first, 8)], stage.at[pl.ds(first, 8)], sem_h.at[t])
 
     def start_load(t, c):
         load(t).start()
         return c
 
+    reads = [
+        pltpu.make_async_copy(src, dst, sem_i.at[n])
+        for n, (src, dst) in enumerate(
+            [(cols_in, cols), (target_in, target), (counts_in, counts), (cond_in, cond), (res_in, res)])
+    ]
+    for read in reads:
+        read.start()
     lax.fori_loop(0, 16, start_load, 0)
-    lane_big = iota((DEVICES, LANES), 1)
-    row_big = iota((DEVICES, LANES), 0)
-    count = jnp.sum(jnp.where(lane_big == row_big, counts[...], 0), axis=1, keepdims=True)
-    count = jnp.broadcast_to(count, (DEVICES, LANES))
-    cntb[...] = count
-    tgt = jnp.where((lane_big < count) & (row_big != me), target[...], -1)
-    trep[...] = lane_pick(tgt, lane_big & (FRONT - 1)).astype(jnp.float32)
-    nxt = lax.rem(me + 1, DEVICES)
-    lane1 = iota((1, LANES), 1)
-    ttsrc[...] = jnp.where((lane1 >= FRONT) & (lane1 < cntb[pl.ds(nxt, 1), :]), target[pl.ds(nxt, 1), :], -1).astype(jnp.float32)
-    own_target = jnp.where(lane1 < cntb[pl.ds(me, 1), :], target[pl.ds(me, 1), :], -1)
-    quarter = lax.shift_right_logical(iota((16, LANES), 1), 5)
-
-    def pack(first):
-        rows = trep[pl.ds(first, 8), :]
-        for e in range(8):
-            x = stage[first + e, 0:16, :]
-            for q in range(1, 4):
-                x = jnp.where(quarter == q, pltpu.roll(stage[first + e, 16 * q : 16 * q + 16, :], 32 * q, 1), x)
-            sbuf[first + e, 0:16, :] = x
-            sbuf[first + e, 16:17, :] = rows[e : e + 1]
-
-    def stamp_copy(d):
-        return pltpu.make_async_remote_copy(
-            src_ref=sbuf.at[d, pl.ds(0, 17)], dst_ref=rbuf_s.at[me, pl.ds(0, 17)], send_sem=sem_ss, recv_sem=sem_rs.at[my_chunk],
-            device_id=(d // NBLK, lax.rem(d, NBLK)), device_id_type=MESH)
-
-    load(0).wait()
-    own_first = pl.multiple_of(my_chunk * 8, 8)
-    pack(own_first)
-    rbuf_s[me] = sbuf[me]
-    pl.semaphore_wait(barrier, DEVICES - 1)
-    for e in range(1, 8):
-        stamp_copy(own_first + lax.rem(me + e, 8)).start()
-
-    def send_chunk(t, c):
-        load(t).wait()
-        first = pl.multiple_of(lax.rem(my_chunk + t, 16) * 8, 8)
-        pack(first)
-        for e in range(8):
-            stamp_copy(first + lax.rem(me + e, 8)).start()
-        return c
-
-    lax.fori_loop(1, 16, send_chunk, 0)
-    tail_dev = (nxt // NBLK, lax.rem(nxt, NBLK))
-    tail_copy = pltpu.make_async_remote_copy(
-        src_ref=stage.at[nxt], dst_ref=tail, send_sem=sem_t.at[0], recv_sem=sem_t.at[1], device_id=tail_dev, device_id_type=MESH)
-    tail_copy.start()
-    ttail_copy = pltpu.make_async_remote_copy(
-        src_ref=ttsrc, dst_ref=ttail, send_sem=sem_t.at[2], recv_sem=sem_t.at[3], device_id=tail_dev, device_id_type=MESH)
-    ttail_copy.start()
+    jac[...] = jnp.zeros_like(jac)
+    us[...] = jnp.zeros_like(us)
+    for read in reads:
+        read.wait()
+    us[0] = -res[...]
 
     owner_row = iota((DEVICES, NBR), 0)
     upper = bf(iota((NBR, NBR), 0) < iota((NBR, NBR), 1))
@@ -241,6 +211,74 @@
     req_src[...] = wanted.astype(jnp.int32)
     lst[...] = (lax.shift_right_logical(iota((8, NBR), 1), 4) * NBR + listed.astype(jnp.int32))[0:1]
 
+    for q in range(16):
+        half = slice(q % 2 * LANES, (q % 2 + 1) * LANES)
+        if q < 14:
+            idx = cols[1 + q // 2 : 2 + q // 2, half] - g * (NBLK * NBR)
+        else:
+            idx = lst[:, half]
+        idx = jnp.broadcast_to(idx, (8, LANES))
+        idx_lo[q] = idx & 127
+        idx_hi[q] = lax.shift_right_logical(idx, 7)
+        idx = jnp.broadcast_to(pidx[q // 2 : q // 2 + 1, half], (8, LANES))
+        far_lo[q] = idx & 127
+        far_hi[q] = lax.shift_right_logical(idx, 7)
+
+    lane_big = iota((DEVICES, LANES), 1)
+    row_big = iota((DEVICES, LANES), 0)
+    count = jnp.sum(jnp.where(lane_big == row_big, counts[...], 0), axis=1, keepdims=True)
+    count = jnp.broadcast_to(count, (DEVICES, LANES))
+    cntb[...] = count
+    tgt = jnp.where((lane_big < count) & (row_big != me), target[...], -1)
+    trep[...] = lane_pick(tgt, lane_big & (FRONT - 1)).astype(jnp.float32)
+    nxt = (me + 1) & (DEVICES - 1)
+    lane1 = iota((1, LANES), 1)
+    ttsrc[...] = jnp.where((lane1 >= FRONT) & (lane1 < cntb[pl.ds(nxt, 1), :]), target[pl.ds(nxt, 1), :], -1).astype(jnp.float32)
+    own_target = jnp.where(lane1 < cntb[pl.ds(me, 1), :], target[pl.ds(me, 1), :], -1)
+    quarter = lax.shift_right_logical(iota((16, LANES), 1), 5)
+
+    def pack(t, c):
+        load(t).wait()
+        first = pl.multiple_of(((my_chunk + t) & 15) * 8, 8)
+        rows = trep[pl.ds(first, 8), :]
+        for e in range(8):
+            x = stage[first + e, 0:16, :]
+            for q in range(1, 4):
+                x = jnp.where(quarter == q, pltpu.roll(stage[first + e, 16 * q : 16 * q + 16, :], 32 * q, 1), x)
+            sbuf[first + e, 0:16, :] = x
+            sbuf[first + e, 16:17, :] = rows[e : e + 1]
+        return c
+
+    lax.fori_loop(0, 16, pack, 0)
+    rbuf_s[me] = sbuf[me]
+    own_first = pl.multiple_of(my_chunk * 8, 8)
+    pl.semaphore_wait(barrier, DEVICES - 1)
+
+    tail_dev = (nxt // NBLK, nxt & (NBLK - 1))
+    tail_copy = pltpu.make_async_remote_copy(
+        src_ref=stage.at[nxt], dst_ref=tail, send_sem=sem_t.at[0], recv_sem=sem_t.at[1], device_id=tail_dev, device_id_type=MESH)
+    tail_copy.start()
+    ttail_copy = pltpu.make_async_remote_copy(
+        src_ref=ttsrc, dst_ref=ttail, send_sem=sem_t.at[2], recv_sem=sem_t.at[3], device_id=tail_dev, device_id_type=MESH)
+    ttail_copy.start()
+
+    def stamp_copy(d):
+        return pltpu.make_async_remote_copy(
+            src_ref=sbuf.at[d, pl.ds(0, 17)], dst_ref=rbuf_s.at[me, pl.ds(0, 17)], send_sem=sem_ss, recv_sem=sem_rs.at[my_chunk],
+            device_id=(d // NBLK, d & (NBLK - 1)), device_id_type=MESH)
+
+    in_chunk = (6, 2, 7, 5, 1, 3, 4, 0)
+
+    def send_chunk(t, c):
+        first = chunk_at(t) * 8
+        for e in in_chunk:
+            stamp_copy(first + ((me ^ e) & 7)).start()
+        return c
+
+    lax.fori_loop(0, 15, send_chunk, 0)
+    for e in in_chunk[:7]:
+        stamp_copy(own_first + ((me ^ e) & 7)).start()
+
     def ask(t, c):
         dg, di = far_dev(t)
         d = dg * NBLK + di
@@ -250,8 +288,6 @@
         return c
 
     lax.fori_loop(0, 112, ask, 0)
-    us[...] = jnp.zeros_like(us)
-    us[0] = -res[...]
     rsrc[...] = jnp.zeros_like(rsrc)
 
     def whole(ref, rows, send, recv):
@@ -259,7 +295,6 @@
             src_ref=ref.at[pl.ds(0, rows)], dst_ref=ref.at[pl.ds(0, rows)], send_sem=send, recv_sem=recv,
             device_id=mate(1), device_id_type=MESH)
 
-    jac[...] = jnp.zeros_like(jac)
     node = iota((NBR, NBR), 0)
 
     def add_slots(values, goal):
@@ -299,22 +334,21 @@
             src_ref=sbuf.at[pl.ds(0, count), pl.ds(0, 17)], dst_ref=rbuf_s.at[pl.ds(0, count), pl.ds(0, 17)],
             send_sem=sem_ss, recv_sem=sem, device_id=mate(1), device_id_type=MESH)
 
-    chunk_wait(own_first, 7, sem_rs.at[my_chunk]).wait_recv()
-    add_chunk(own_first)
-
-    def take_chunk(t, c):
-        chunk = lax.rem(my_chunk + 16 - t, 16)
-        first = pl.multiple_of(chunk * 8, 8)
-        chunk_wait(first, 8, sem_rs.at[chunk]).wait_recv()
-        add_chunk(first)
-        return c
-
-    lax.fori_loop(1, 16, take_chunk, 0)
     tail_copy.wait_recv()
     ttail_copy.wait_recv()
     add_slots(
         jnp.concatenate([stage[me], tail[...]], axis=1),
         jnp.concatenate([own_target, ttail[...].astype(jnp.int32)], axis=1))
+    def take_chunk(t, c):
+        chunk = chunk_at(t)
+        first = pl.multiple_of(chunk * 8, 8)
+        chunk_wait(first, 8, sem_rs.at[chunk]).wait_recv()
+        add_chunk(first)
+        return c
+
+    lax.fori_loop(0, 15, take_chunk, 0)
+    chunk_wait(own_first, 7, sem_rs.at[my_chunk]).wait_recv()
+    add_chunk(own_first)
     sub8 = iota((8, NBR), 0)
     for a in range(8):
         jac[0, a] = jac[0, a] + jnp.where(sub8 == a, jnp.broadcast_to(cond[a : a + 1, :], (8, NBR)), 0.0)
@@ -341,34 +375,39 @@
     asked.wait_recv()
     asked.wait_send()
 
-    order = (10, 9, 11, 6, 14, 5, 7, 13, 15, 2, 8, 1, 3, 4, 12)
+    y, z_at = i // 4, i & 3
+    by_hops = [[] for _ in range(5)]
+    for oy in range(4):
+        for oz in range(4):
+            by_hops[min(oy, 4 - oy) + min(oz, 4 - oz)].append((oy, oz))
 
     def spread(buf, send, recv):
-        for o in order:
-            y, z = i // 4, lax.rem(i, 4)
-            to = lax.rem(y + o // 4, 4) * 4 + lax.rem(z + o % 4, 4)
-            pltpu.make_async_remote_copy(
-                src_ref=buf.at[i], dst_ref=buf.at[i], send_sem=send, recv_sem=recv,
-                device_id=(g, to), device_id_type=MESH).start()
-
-    def near_pick(buf):
-        picked = []
-        for q in range(16):
-            if q < 14:
-                idx = cols[1 + q // 2 : 2 + q // 2, q % 2 * LANES : (q % 2 + 1) * LANES] - g * (NBLK * NBR)
-            else:
-                idx = lst[:, (q - 14) * LANES : (q - 13) * LANES]
-            idx = jnp.broadcast_to(idx, (8, LANES))
-            lo, hi = idx & 127, lax.shift_right_logical(idx, 7)
-            acc = jnp.zeros((8, LANES), jnp.float32)
-            for v in range(32):
-                acc = jnp.where(hi == v, lane_pick(buf[v // 2, :, v % 2 * LANES : (v % 2 + 1) * LANES], lo), acc)
-            picked.append(acc)
-        return picked
-
-    def far_place(q):
-        idx = jnp.broadcast_to(pidx[q // 2 : q // 2 + 1, q % 2 * LANES : (q % 2 + 1) * LANES], (8, LANES))
-        return idx & 127, lax.shift_right_logical(idx, 7)
+        for hops in (4, 3, 2, 1):
+            for oy, oz in by_hops[hops]:
+                to = ((y + oy) & 3) * 4 + ((z_at + oz) & 3)
+                pltpu.make_async_remote_copy(
+                    src_ref=buf.at[i], dst_ref=buf.at[i], send_sem=send, recv_sem=recv.at[hops],
+                    device_id=(g, to), device_id_type=MESH).start()
+
+    def sent(buf, send, recv):
+        whole(buf, 15, send, recv.at[0]).wait_send()
+
+    def near_pick(buf, send, recv):
+        acc = [jnp.zeros((8, LANES), jnp.float32)] * 16
+        for part in ((0, 1, 2, 3), (4,)):
+            tables = []
+            for hops in part:
+                if hops:
+                    whole(buf, len(by_hops[hops]), send, recv.at[hops]).wait_recv()
+                for oy, oz in by_hops[hops]:
+                    tables.append(((y - oy) & 3) * 4 + ((z_at - oz) & 3))
+            for q in range(16):
+                lo, hi, x = idx_lo[q], idx_hi[q], acc[q]
+                for s in tables:
+                    for h in range(2):
+                        x = jnp.where(hi == 2 * s + h, lane_pick(buf[s, :, h * LANES : (h + 1) * LANES], lo), x)
+                acc[q] = x
+        return acc
 
     def add_slot(acc, k, picked):
         return [x + jac[k, a] * picked for a, x in enumerate(acc)]
@@ -376,18 +415,17 @@
     def joined(first, second):
         return jnp.concatenate([first, second], axis=1)
 
-    def near_couple(buf):
-        picked = near_pick(buf)
+    def near_couple(buf, send, recv):
+        picked = near_pick(buf, send, recv)
         acc = [jnp.zeros((8, NBR), jnp.float32)] * 8
         for k in range(7):
             acc = add_slot(acc, 1 + k, joined(picked[2 * k], picked[2 * k + 1]))
         for k in range(8):
             got = []
             for h in range(2):
-                lo, hi = far_place(2 * k + h)
                 x = jnp.zeros((8, LANES), jnp.float32)
                 for v in range(2):
-                    x = jnp.where(hi == 2 * g + v, lane_pick(picked[14 + v], lo), x)
+                    x = jnp.where(far_hi[2 * k + h] == 2 * g + v, lane_pick(picked[14 + v], far_lo[2 * k + h]), x)
                 got.append(x)
             acc = add_slot(acc, 8 + k, joined(*got))
         return fold_rows(acc)
@@ -395,9 +433,11 @@
     lane16 = iota((8, LANES), 1) & 15
     lane_group = lax.shift_right_logical(iota((8, LANES), 1), 4)
     turn = iota((8, LANES), 0) * 16 + lane16
+    x_at, core = g // 2, g & 1
+    far_groups = [[(0, 1)], [(1, 0), (1, 1), (3, 0), (3, 1)], [(2, 0), (2, 1)]]
 
     def step(j, carry):
-        slot = lax.rem(j, 2)
+        slot = j & 1
         u = us[j]
         z = block_mul(dinv, u)
         buf_a[i, :, 0:NBR] = z
@@ -410,8 +450,9 @@
             dots.append(t[:, :LANES] + t[:, LANES:])
         zero = jnp.zeros((8, LANES), jnp.float32)
         gp[j] = fold_rows(dots + [zero, zero])
-        done_a = whole(buf_a, 15, sem_sa, sem_ra)
-        done_a.wait_recv()
+        z = block_mul(dinv, u - near_couple(buf_a, sem_sa, sem_ra))
+        buf_b[i] = z
+        spread(buf_b, sem_sb, sem_rb)
         nsum = buf_a[0, :, NBR : NBR + LANES]
         for s in range(1, NBLK):
             nsum = nsum + buf_a[s, :, NBR : NBR + LANES]
@@ -422,84 +463,90 @@
                 src_ref=nsrc, dst_ref=nbuf.at[slot, g], send_sem=sem_sn.at[slot], recv_sem=sem_rn.at[slot],
                 device_id=peer(o), device_id_type=MESH).start()
         nbuf[slot, g] = nrow
-        coupled = near_couple(buf_a)
-        z = block_mul(dinv, u - coupled)
-        done_a.wait_send()
-        buf_b[i] = z
-        spread(buf_b, sem_sb, sem_rb)
-        done_b = whole(buf_b, 15, sem_sb, sem_rb)
-        done_b.wait_recv()
-        coupled = near_couple(buf_b)
-        z = block_mul(dinv, u - coupled)
-        done_b.wait_send()
+        sent(buf_a, sem_sa, sem_ra)
+        z = block_mul(dinv, u - near_couple(buf_b, sem_sb, sem_rb))
         buf_c[i] = z
-        def far_send(t, c):
-            dg = lax.rem(g + 1 + t // 2, NGRP)
-            first = pl.multiple_of(dg * NBLK + lax.rem(t, 2) * 8, 8)
+
+        def far_send(dx, dc, half):
+            dg = ((x_at + dx) & 3) * 2 + (core ^ dc)
+            first = pl.multiple_of(dg * NBLK + half * 8, 8)
             idx = req[pl.ds(first, 8), :]
             lo, hi = idx & 127, lax.shift_right_logical(idx, 7)
             out = jnp.zeros((8, LANES), jnp.float32)
             for b in range(8):
                 for h in range(2):
-                    table = jnp.broadcast_to(buf_c[i, b : b + 1, h * LANES : (h + 1) * LANES], (8, LANES))
+                    table = jnp.broadcast_to(z[b : b + 1, h * LANES : (h + 1) * LANES], (8, LANES))
                     out = jnp.where((hi == h) & (lane_group == b), lane_pick(table, lo), out)
             fsrc[pl.ds(first, 8), :] = out
             for d in range(8):
                 pltpu.make_async_remote_copy(
                     src_ref=fsrc.at[pl.ds(first + d, 1)], dst_ref=fbuf.at[slot, pl.ds(me, 1)],
-                    send_sem=sem_sf, recv_sem=sem_rf.at[slot],
-                    device_id=(dg, lax.rem(t, 2) * 8 + d), device_id_type=MESH).start()
-            return c
-
+                    send_sem=sem_sf, recv_sem=sem_rf.at[slot, {0: 0, 1: 1, 3: 1, 2: 2}[dx]],
+                    device_id=(dg, half * 8 + d), device_id_type=MESH).start()
+
+        for dx, dc in far_groups[2]:
+            for half in range(2):
+                far_send(dx, dc, half)
         spread(buf_c, sem_sc, sem_rc)
-        lax.fori_loop(0, 14, far_send, 0)
+        for dx, dc in far_groups[1] + far_groups[0]:
+            for half in range(2):
+                far_send(dx, dc, half)
+        sent(buf_b, sem_sb, sem_rb)
         ss[j] = z
-        base = [jac[0, a] * z for a in range(8)]
-        done_c = whole(buf_c, 15, sem_sc, sem_rc)
-        done_c.wait_recv()
-        picked = near_pick(buf_c)
-        acc = base
+        acc = [jac[0, a] * z for a in range(8)]
+        picked = near_pick(buf_c, sem_sc, sem_rc)
         for k in range(7):
             acc = add_slot(acc, 1 + k, joined(picked[2 * k], picked[2 * k + 1]))
-        done_c.wait_send()
-        done_f = pltpu.make_async_remote_copy(
-            src_ref=fsrc.at[pl.ds(0, 112)], dst_ref=fbuf.at[slot, pl.ds(0, 112)], send_sem=sem_sf, recv_sem=sem_rf.at[slot],
-            device_id=mate(1), device_id_type=MESH)
-        done_f.wait_recv()
-        for q in range(16):
-            x = jnp.zeros((8, LANES), jnp.float32)
-            for o in range(8):
-                rowv = jnp.broadcast_to(fbuf[slot, 8 * q + o : 8 * q + o + 1, :], (8, LANES))
-                x = jnp.where(lane_group == o, lane_pick(rowv, turn), x)
-            fpk[q] = x
-        fpk[2 * g] = picked[14]
-        fpk[2 * g + 1] = picked[15]
+        got = [jnp.zeros((8, LANES), jnp.float32)] * 16
+
+        def place_far(tables):
+            for q in range(16):
+                lo, hi, x = far_lo[q], far_hi[q], got[q]
+                for at, table in tables:
+                    x = jnp.where(hi == at, lane_pick(table, lo), x)
+                got[q] = x
+
+        place_far([(2 * g + v, picked[14 + v]) for v in range(2)])
+        sent(buf_c, sem_sc, sem_rc)
+
+        def far_part(count, cls):
+            return pltpu.make_async_remote_copy(
+                src_ref=fsrc.at[pl.ds(0, count)], dst_ref=fbuf.at[slot, pl.ds(0, count)], send_sem=sem_sf,
+                recv_sem=sem_rf.at[slot, cls], device_id=mate(1), device_id_type=MESH)
+
+        for cls, groups in enumerate(far_groups):
+            far_part(16 * len(groups), cls).wait_recv()
+            tables = []
+            for dx, dc in groups:
+                dg = ((x_at + dx) & 3) * 2 + (core ^ dc)
+                for half in range(2):
+                    rows = fbuf[slot, pl.ds(pl.multiple_of(dg * NBLK + half * 8, 8), 8), :]
+                    table = jnp.zeros((8, LANES), jnp.float32)
+                    for o in range(8):
+                        table = jnp.where(lane_group == o, lane_pick(jnp.broadcast_to(rows[o : o + 1], (8, LANES)), turn), table)
+                    tables.append((2 * dg + half, table))
+            place_far(tables)
         for k in range(8):
-            got = []
-            for h in range(2):
-                lo, hi = far_place(2 * k + h)
-                x = jnp.zeros((8, LANES), jnp.float32)
-                for v in range(16):
-                    x = jnp.where(hi == v, lane_pick(fpk[v], lo), x)
-                got.append(x)
-            acc = add_slot(acc, 8 + k, joined(*got))
+            acc = add_slot(acc, 8 + k, joined(got[2 * k], got[2 * k + 1]))
         image = fold_rows(acc)
-        done_f.wait_send()
         done_n = pltpu.make_async_remote_copy(
             src_ref=nbuf.at[slot, pl.ds(0, 7)], dst_ref=nbuf.at[slot, pl.ds(0, 7)], send_sem=sem_sn.at[slot], recv_sem=sem_rn.at[slot],
             device_id=mate(1), device_id_type=MESH)
         done_n.wait_recv()
-        done_n.wait_send()
         total = nbuf[slot, 0]
         for s in range(1, NGRP):
             total = total + nbuf[slot, s]
         scale = lax.rsqrt(jnp.maximum(jnp.sum(total, axis=1, keepdims=True), 1e-12))
         sig[j] = jnp.broadcast_to(scale, (8, LANES))
         us[j + 1] = (image - u) * scale
+        done_n.wait_send()
+        far_part(112, 0).wait_send()
         return carry
 
     lax.fori_loop(0, KRYLOV, step, 0)
 
+    pre_copy = pltpu.make_async_copy(ss.at[0], pre_out, sem_o.at[0])
+    pre_copy.start()
     u = us[KRYLOV]
     dots = []
     for l in range(6):
@@ -515,16 +562,16 @@
         row = row + jnp.sum(jnp.where(lane == 8 * j + sub, s, 0.0), axis=0, keepdims=True)
     rsrc[...] = row
 
-    def tell(o, c):
-        d = lax.rem(me + o, DEVICES)
+    def tell(t, c):
+        d = farthest_first(t)
         pltpu.make_async_remote_copy(
-            src_ref=rsrc, dst_ref=rbuf.at[pl.ds(me, 1)], send_sem=sem_sf, recv_sem=sem_rf.at[2],
-            device_id=(d // NBLK, lax.rem(d, NBLK)), device_id_type=MESH).start()
+            src_ref=rsrc, dst_ref=rbuf.at[pl.ds(me, 1)], send_sem=sem_sf, recv_sem=sem_rf.at[2, 0],
+            device_id=(d // NBLK, d & (NBLK - 1)), device_id_type=MESH).start()
         return c
 
-    lax.fori_loop(1, DEVICES, tell, 0)
+    lax.fori_loop(0, DEVICES - 1, tell, 0)
     rbuf[pl.ds(me, 1), :] = row
-    done = whole(rbuf, 127, sem_sf, sem_rf.at[2])
+    done = whole(rbuf, 127, sem_sf, sem_rf.at[2, 0])
     done.wait_recv()
     done.wait_send()
     total = rbuf[0:8, :]
@@ -539,25 +586,55 @@
         for l in range(1, KRYLOV):
             x = x + weights[l] * ss[l, :, part]
         upd[:, part] = x
-    pre[...] = ss[0]
+    upd_copy = pltpu.make_async_copy(upd, upd_out, sem_o.at[1])
+    upd_copy.start()
     jac_copy.wait()
+    pre_copy.wait()
+    upd_copy.wait()
+
+
+def hand_on(upd_in, jac_in, pre_in, upd, jac, pre, upd_v, jac_v, pre_v, sem_in, sem_out):
+    parts = [(upd_in, upd_v, upd), (pre_in, pre_v, pre)]
+    for n in range(0, K, 4):
+        part = pl.ds(n, 4)
+        parts.append((jac_in.at[part], jac_v.at[part], jac.at[part]))
+    reads = [pltpu.make_async_copy(src, mid, sem_in.at[n]) for n, (src, mid, _) in enumerate(parts)]
+    writes = [pltpu.make_async_copy(mid, dst, sem_out.at[n]) for n, (_, mid, dst) in enumerate(parts)]
+    for read in reads:
+        read.start()
+    for read, write in zip(reads, writes):
+        read.wait()
+        write.start()
+    for write in writes:
+        write.wait()
 
 
 def local(stamps, stamp_target, pair_counts, conductance, block_cols, newton_residual):
-    vm = pl.BlockSpec(memory_space=pltpu.VMEM)
     hbm = pl.BlockSpec(memory_space=pl.ANY)
     f32, i32 = jnp.float32, jnp.int32
     dma = pltpu.SemaphoreType.DMA
-    return pl.pallas_call(
-        solver_kernel,
-        out_shape=(
+    shapes = (
             jax.ShapeDtypeStruct((8, NBR), f32),
             jax.ShapeDtypeStruct((K, 8, 8, NBR), f32),
             jax.ShapeDtypeStruct((8, NBR), f32),
-        ),
-        in_specs=[hbm] + [vm] * 5,
-        out_specs=(vm, hbm, vm),
+    )
+    results = pl.pallas_call(
+        solver_kernel,
+        out_shape=shapes,
+        in_specs=[hbm] * 6,
+        out_specs=(hbm, hbm, hbm),
         scratch_shapes=[
+            pltpu.VMEM((DEVICES, LANES), i32),
+            pltpu.VMEM((1, LANES), i32),
+            pltpu.VMEM((8, NBR), f32),
+            pltpu.VMEM((8, NBR), f32),
+            pltpu.VMEM((K, NBR), i32),
+            pltpu.VMEM((8, NBR), f32),
+            pltpu.VMEM((16, 8, LANES), i32),
+            pltpu.VMEM((16, 8, LANES), i32),
+            pltpu.VMEM((16, 8, LANES), i32),
+            pltpu.VMEM((16, 8, LANES), i32),
+            dma((5,)), dma((2,)),
             pltpu.VMEM((DEVICES, 64, LANES), f32),
             pltpu.VMEM((DEVICES, 24, LANES), f32),
             pltpu.VMEM((DEVICES, 24, LANES), f32),
@@ -586,11 +663,20 @@
             pltpu.VMEM((KRYLOV, 8, LANES), f32),
             pltpu.VMEM((8, NBR), i32),
             pltpu.VMEM((1, NBR), i32),
-            pltpu.VMEM((16, 8, LANES), f32),
-            dma, dma, dma, dma, dma((3,)), dma, dma, dma, dma((3,)), dma((3,)),
+            dma, dma, dma, dma, dma((3,)), dma((5,)), dma((5,)), dma((5,)), dma((3, 3)), dma((3,)),
         ],
-        compiler_params=pltpu.CompilerParams(collective_id=0, has_side_effects=True, vmem_limit_bytes=48 * 1024 * 1024),
+        compiler_params=pltpu.CompilerParams(collective_id=0, has_side_effects=True, vmem_limit_bytes=62 * 1024 * 1024),
     )(stamps, stamp_target.reshape(DEVICES, LANES), pair_counts, conductance, newton_residual, block_cols)
+    return pl.pallas_call(
+        hand_on,
+        out_shape=shapes,
+        in_specs=[hbm] * 3,
+        out_specs=(hbm, hbm, hbm),
+        scratch_shapes=[
+            pltpu.VMEM((8, NBR), f32), pltpu.VMEM((K, 8, 8, NBR), f32), pltpu.VMEM((8, NBR), f32), dma((6,)), dma((6,)),
+        ],
+        compiler_params=pltpu.CompilerParams(vmem_limit_bytes=62 * 1024 * 1024),
+    )(*results)
 
 
 def solution(mesh):

time: 145 us -> 140 us (0.966)
  local copies, waits for them, and re-layouts: 7.95 us -> 0 us
  Pallas kernels: 136 us -> 140 us
    unnamed x15 -> x0, local copies, waits for them, and re-layouts: 7.95 us -> none
    pallas_call x1 -> x2, Pallas kernels: 136 us -> 140 us  [the longest x1 138 us: local(): pl.pallas_call(solver_kernel, out_shape=shapes, in_specs=[hbm] * 6, out_s...]
where the time goes in v3:
time: 140 us
  Pallas kernels  140 us (100%)
    pallas_call x1, Pallas kernels, local(): pl.pallas_call(solver_kernel, out_shape=shapes, in_specs=[hbm] * 6, out_s...  138 us

profile of v3, /device:TPU:1, one launch (start us, length us, event | category | flops | bytes accessed | tf_op | source)
XLA Modules:
  0.0 140.3 jit_solution(2190876882768992754)
XLA Ops:
  0.6 137.6 %shard_map.85 = (f32[8,256]{1,0:T(8,128)}, f32[16,8,8,256]{3,2,1,0:T(8,128)}, f32[8,256]{1,0:T(8,128)}) custom-call(f32[1,128,64,128]{3,2,1,0:T(8,128)} %stamps.1, s32[128,128]{1,0:T(8,128)} %bitcast.1, s32[1,128]{1,0:T(1,128)} %counts_in.1, f32[8,256]{1,0:T(8,128)} %cond_in.1, f32[8,256]{1,0:T(8,128)} %res_in.1, s32[16,256]{1,0:T(8,128)} %cols_in.1), custom_call_target="tpu_custom_call" | custom-call | tf_op jit(solution)/shard_map/pallas_call | solution.py:621
  138.2 2.0 %shard_map.86 = (f32[8,256]{1,0:T(8,128)}, f32[16,8,8,256]{3,2,1,0:T(8,128)}, f32[8,256]{1,0:T(8,128)}) custom-call(f32[8,256]{1,0:T(8,128)} %get-tuple-element.6.upd_in, f32[16,8,8,256]{3,2,1,0:T(8,128)} %get-tuple-element.7.jac_in, f32[8,256]{1,0:T(8,128)} %get-tuple-element.8.pre_in), custom_call_target="tpu_custom_call" | custom-call | tf_op jit(solution)/shard_map/pallas_call | solution.py:670

commit v4 on v3

--- a/solution.py
+++ b/solution.py
@@ -127,7 +127,7 @@
 
 
 def solver_kernel(stamps, target_in, counts_in, cond_in, res_in, cols_in, upd_out, jac_out, pre_out,
-                  target, counts, cond, res, cols, upd, idx_lo, idx_hi, far_lo, far_hi, sem_i, sem_o,
+                  target, counts, cond, res, cols, upd, idx_lo, idx_hi, far_lo, far_hi, gbuf, sem_g, sem_i, sem_o,
                   stage, sbuf, rbuf_s, trep, cntb, tail, ttail, ttsrc, jac, dinv, sem_h, sem_ss, sem_rs, sem_t, sem_j,
                   buf_a, buf_b, buf_c, fsrc, fbuf, req_src, req, nsrc, nbuf, rsrc, rbuf,
                   us, ss, gp, sig, pidx, lst,
@@ -184,6 +184,62 @@
     for read in reads:
         read.wait()
     us[0] = -res[...]
+
+    nt = (((1,), (1,)), ((), ()))
+    lane_big = iota((DEVICES, LANES), 1)
+    row_big = iota((DEVICES, LANES), 0)
+    count = jnp.sum(jnp.where(lane_big == row_big, counts[...], 0), axis=1, keepdims=True)
+    count = jnp.broadcast_to(count, (DEVICES, LANES))
+    cntb[...] = count
+    tgt = jnp.where((lane_big < count) & (row_big != me), target[...], -1)
+    trep[...] = lane_pick(tgt, lane_big & (FRONT - 1)).astype(jnp.float32)
+    nxt = (me + 1) & (DEVICES - 1)
+    lane1 = iota((1, LANES), 1)
+    ttsrc[...] = jnp.where((lane1 >= FRONT) & (lane1 < cntb[pl.ds(nxt, 1), :]), target[pl.ds(nxt, 1), :], -1).astype(jnp.float32)
+    own_target = jnp.where(lane1 < cntb[pl.ds(me, 1), :], target[pl.ds(me, 1), :], -1)
+    quarter = lax.shift_right_logical(iota((16, LANES), 1), 5)
+
+    def pack(t, c):
+        load(t).wait()
+        first = pl.multiple_of(((my_chunk + t) & 15) * 8, 8)
+        rows = trep[pl.ds(first, 8), :]
+        for e in range(8):
+            x = stage[first + e, 0:16, :]
+            for q in range(1, 4):
+                x = jnp.where(quarter == q, pltpu.roll(stage[first + e, 16 * q : 16 * q + 16, :], 32 * q, 1), x)
+            sbuf[first + e, 0:16, :] = x
+            sbuf[first + e, 16:17, :] = rows[e : e + 1]
+        return c
+
+    lax.fori_loop(0, 16, pack, 0)
+    rbuf_s[me] = sbuf[me]
+    own_first = pl.multiple_of(my_chunk * 8, 8)
+    pl.semaphore_wait(barrier, DEVICES - 1)
+
+    tail_dev = (nxt // NBLK, nxt & (NBLK - 1))
+    tail_copy = pltpu.make_async_remote_copy(
+        src_ref=stage.at[nxt], dst_ref=tail, send_sem=sem_t.at[0], recv_sem=sem_t.at[1], device_id=tail_dev, device_id_type=MESH)
+    tail_copy.start()
+    ttail_copy = pltpu.make_async_remote_copy(
+        src_ref=ttsrc, dst_ref=ttail, send_sem=sem_t.at[2], recv_sem=sem_t.at[3], device_id=tail_dev, device_id_type=MESH)
+    ttail_copy.start()
+
+    def stamp_copy(d):
+        return pltpu.make_async_remote_copy(
+            src_ref=sbuf.at[d, pl.ds(0, 17)], dst_ref=rbuf_s.at[me, pl.ds(0, 17)], send_sem=sem_ss, recv_sem=sem_rs.at[my_chunk],
+            device_id=(d // NBLK, d & (NBLK - 1)), device_id_type=MESH)
+
+    in_chunk = (6, 2, 7, 5, 1, 3, 4, 0)
+
+    def send_chunk(t, c):
+        first = chunk_at(t) * 8
+        for e in in_chunk:
+            stamp_copy(first + ((me ^ e) & 7)).start()
+        return c
+
+    lax.fori_loop(0, 15, send_chunk, 0)
+    for e in in_chunk[:7]:
+        stamp_copy(own_first + ((me ^ e) & 7)).start()
 
     owner_row = iota((DEVICES, NBR), 0)
     upper = bf(iota((NBR, NBR), 0) < iota((NBR, NBR), 1))
@@ -224,61 +280,6 @@
         far_lo[q] = idx & 127
         far_hi[q] = lax.shift_right_logical(idx, 7)
 
-    lane_big = iota((DEVICES, LANES), 1)
-    row_big = iota((DEVICES, LANES), 0)
-    count = jnp.sum(jnp.where(lane_big == row_big, counts[...], 0), axis=1, keepdims=True)
-    count = jnp.broadcast_to(count, (DEVICES, LANES))
-    cntb[...] = count
-    tgt = jnp.where((lane_big < count) & (row_big != me), target[...], -1)
-    trep[...] = lane_pick(tgt, lane_big & (FRONT - 1)).astype(jnp.float32)
-    nxt = (me + 1) & (DEVICES - 1)
-    lane1 = iota((1, LANES), 1)
-    ttsrc[...] = jnp.where((lane1 >= FRONT) & (lane1 < cntb[pl.ds(nxt, 1), :]), target[pl.ds(nxt, 1), :], -1).astype(jnp.float32)
-    own_target = jnp.where(lane1 < cntb[pl.ds(me, 1), :], target[pl.ds(me, 1), :], -1)
-    quarter = lax.shift_right_logical(iota((16, LANES), 1), 5)
-
-    def pack(t, c):
-        load(t).wait()
-        first = pl.multiple_of(((my_chunk + t) & 15) * 8, 8)
-        rows = trep[pl.ds(first, 8), :]
-        for e in range(8):
-            x = stage[first + e, 0:16, :]
-            for q in range(1, 4):
-                x = jnp.where(quarter == q, pltpu.roll(stage[first + e, 16 * q : 16 * q + 16, :], 32 * q, 1), x)
-            sbuf[first + e, 0:16, :] = x
-            sbuf[first + e, 16:17, :] = rows[e : e + 1]
-        return c
-
-    lax.fori_loop(0, 16, pack, 0)
-    rbuf_s[me] = sbuf[me]
-    own_first = pl.multiple_of(my_chunk * 8, 8)
-    pl.semaphore_wait(barrier, DEVICES - 1)
-
-    tail_dev = (nxt // NBLK, nxt & (NBLK - 1))
-    tail_copy = pltpu.make_async_remote_copy(
-        src_ref=stage.at[nxt], dst_ref=tail, send_sem=sem_t.at[0], recv_sem=sem_t.at[1], device_id=tail_dev, device_id_type=MESH)
-    tail_copy.start()
-    ttail_copy = pltpu.make_async_remote_copy(
-        src_ref=ttsrc, dst_ref=ttail, send_sem=sem_t.at[2], recv_sem=sem_t.at[3], device_id=tail_dev, device_id_type=MESH)
-    ttail_copy.start()
-
-    def stamp_copy(d):
-        return pltpu.make_async_remote_copy(
-            src_ref=sbuf.at[d, pl.ds(0, 17)], dst_ref=rbuf_s.at[me, pl.ds(0, 17)], send_sem=sem_ss, recv_sem=sem_rs.at[my_chunk],
-            device_id=(d // NBLK, d & (NBLK - 1)), device_id_type=MESH)
-
-    in_chunk = (6, 2, 7, 5, 1, 3, 4, 0)
-
-    def send_chunk(t, c):
-        first = chunk_at(t) * 8
-        for e in in_chunk:
-            stamp_copy(first + ((me ^ e) & 7)).start()
-        return c
-
-    lax.fori_loop(0, 15, send_chunk, 0)
-    for e in in_chunk[:7]:
-        stamp_copy(own_first + ((me ^ e) & 7)).start()
-
     def ask(t, c):
         dg, di = far_dev(t)
         d = dg * NBLK + di
@@ -440,10 +441,14 @@
         slot = j & 1
         u = us[j]
         z = block_mul(dinv, u)
-        buf_a[i, :, 0:NBR] = z
+        buf_a[i] = z
+        spread(buf_a, sem_sa, sem_ra)
         sq = u * u
-        buf_a[i, :, NBR : NBR + LANES] = sq[:, :LANES] + sq[:, LANES:]
-        spread(buf_a, sem_sa, sem_ra)
+        gbuf[i] = jnp.sum(sq[:, :LANES] + sq[:, LANES:], axis=0, keepdims=True)
+        for o in range(1, NBLK):
+            pltpu.make_async_remote_copy(
+                src_ref=gbuf.at[i], dst_ref=gbuf.at[i], send_sem=sem_g.at[0], recv_sem=sem_g.at[1],
+                device_id=mate(o), device_id_type=MESH).start()
         dots = []
         for l in range(6):
             t = u * us[l]
@@ -453,16 +458,18 @@
         z = block_mul(dinv, u - near_couple(buf_a, sem_sa, sem_ra))
         buf_b[i] = z
         spread(buf_b, sem_sb, sem_rb)
-        nsum = buf_a[0, :, NBR : NBR + LANES]
+        done_g = whole(gbuf, 15, sem_g.at[0], sem_g.at[1])
+        done_g.wait_recv()
+        nrow = gbuf[0]
         for s in range(1, NBLK):
-            nsum = nsum + buf_a[s, :, NBR : NBR + LANES]
-        nrow = jnp.sum(nsum, axis=0, keepdims=True)
+            nrow = nrow + gbuf[s]
         nsrc[...] = nrow
         for o in range(1, NGRP):
             pltpu.make_async_remote_copy(
                 src_ref=nsrc, dst_ref=nbuf.at[slot, g], send_sem=sem_sn.at[slot], recv_sem=sem_rn.at[slot],
                 device_id=peer(o), device_id_type=MESH).start()
         nbuf[slot, g] = nrow
+        done_g.wait_send()
         sent(buf_a, sem_sa, sem_ra)
         z = block_mul(dinv, u - near_couple(buf_b, sem_sb, sem_rb))
         buf_c[i] = z
@@ -634,7 +641,8 @@
             pltpu.VMEM((16, 8, LANES), i32),
             pltpu.VMEM((16, 8, LANES), i32),
             pltpu.VMEM((16, 8, LANES), i32),
-            dma((5,)), dma((2,)),
+            pltpu.VMEM((NBLK, 1, LANES), f32),
+            dma((2,)), dma((5,)), dma((2,)),
             pltpu.VMEM((DEVICES, 64, LANES), f32),
             pltpu.VMEM((DEVICES, 24, LANES), f32),
             pltpu.VMEM((DEVICES, 24, LANES), f32),
@@ -646,7 +654,7 @@
             pltpu.VMEM((K, 8, 8, NBR), f32),
             pltpu.VMEM((8, 8, NBR), f32),
             dma((16,)), dma, dma((16,)), dma((4,)), dma,
-            pltpu.VMEM((NBLK, 8, NBR + LANES), f32),
+            pltpu.VMEM((NBLK, 8, NBR), f32),
             pltpu.VMEM((NBLK, 8, NBR), f32),
             pltpu.VMEM((NBLK, 8, NBR), f32),
             pltpu.VMEM((DEVICES, LANES), f32),

time: 140 us -> 137 us (0.979)
  Pallas kernels: 140 us -> 136 us
    pallas_call x1, Pallas kernels: 138 us -> 134 us  [local(): pl.pallas_call(solver_kernel, out_shape=shapes, in_specs=[hbm] * 6, out_s...]
where the time goes in v4:
time: 137 us
  Pallas kernels  136 us (99%)
    pallas_call x1, Pallas kernels, local(): pl.pallas_call(solver_kernel, out_shape=shapes, in_specs=[hbm] * 6, out_s...  134 us

profile of v4, /device:TPU:1, one launch (start us, length us, event | category | flops | bytes accessed | tf_op | source)
XLA Modules:
  0.0 136.7 jit_solution(4139917367909239235)
XLA Ops:
  0.6 134.0 %shard_map.85 = (f32[8,256]{1,0:T(8,128)}, f32[16,8,8,256]{3,2,1,0:T(8,128)}, f32[8,256]{1,0:T(8,128)}) custom-call(f32[1,128,64,128]{3,2,1,0:T(8,128)} %stamps.1, s32[128,128]{1,0:T(8,128)} %bitcast.1, s32[1,128]{1,0:T(1,128)} %counts_in.1, f32[8,256]{1,0:T(8,128)} %cond_in.1, f32[8,256]{1,0:T(8,128)} %res_in.1, s32[16,256]{1,0:T(8,128)} %cols_in.1), custom_call_target="tpu_custom_call" | custom-call | tf_op jit(solution)/shard_map/pallas_call | solution.py:628
  134.6 2.0 %shard_map.86 = (f32[8,256]{1,0:T(8,128)}, f32[16,8,8,256]{3,2,1,0:T(8,128)}, f32[8,256]{1,0:T(8,128)}) custom-call(f32[8,256]{1,0:T(8,128)} %get-tuple-element.6.upd_in, f32[16,8,8,256]{3,2,1,0:T(8,128)} %get-tuple-element.7.jac_in, f32[8,256]{1,0:T(8,128)} %get-tuple-element.8.pre_in), custom_call_target="tpu_custom_call" | custom-call | tf_op jit(solution)/shard_map/pallas_call | solution.py:678

commit v5 on v4

--- a/solution.py
+++ b/solution.py
@@ -521,6 +521,15 @@
                 src_ref=fsrc.at[pl.ds(0, count)], dst_ref=fbuf.at[slot, pl.ds(0, count)], send_sem=sem_sf,
                 recv_sem=sem_rf.at[slot, cls], device_id=mate(1), device_id_type=MESH)
 
+        done_n = pltpu.make_async_remote_copy(
+            src_ref=nbuf.at[slot, pl.ds(0, 7)], dst_ref=nbuf.at[slot, pl.ds(0, 7)], send_sem=sem_sn.at[slot], recv_sem=sem_rn.at[slot],
+            device_id=mate(1), device_id_type=MESH)
+        done_n.wait_recv()
+        total = nbuf[slot, 0]
+        for s in range(1, NGRP):
+            total = total + nbuf[slot, s]
+        scale = lax.rsqrt(jnp.maximum(jnp.sum(total, axis=1, keepdims=True), 1e-12))
+        sig[j] = jnp.broadcast_to(scale, (8, LANES))
         for cls, groups in enumerate(far_groups):
             far_part(16 * len(groups), cls).wait_recv()
             tables = []
@@ -536,15 +545,6 @@
         for k in range(8):
             acc = add_slot(acc, 8 + k, joined(got[2 * k], got[2 * k + 1]))
         image = fold_rows(acc)
-        done_n = pltpu.make_async_remote_copy(
-            src_ref=nbuf.at[slot, pl.ds(0, 7)], dst_ref=nbuf.at[slot, pl.ds(0, 7)], send_sem=sem_sn.at[slot], recv_sem=sem_rn.at[slot],
-            device_id=mate(1), device_id_type=MESH)
-        done_n.wait_recv()
-        total = nbuf[slot, 0]
-        for s in range(1, NGRP):
-            total = total + nbuf[slot, s]
-        scale = lax.rsqrt(jnp.maximum(jnp.sum(total, axis=1, keepdims=True), 1e-12))
-        sig[j] = jnp.broadcast_to(scale, (8, LANES))
         us[j + 1] = (image - u) * scale
         done_n.wait_send()
         far_part(112, 0).wait_send()

time: 137 us -> 137 us (level)
  no operation moved by 1% of the time
where the time goes in v5:
time: 137 us; the launch traced here: 136 us
  Pallas kernels  136 us (99%)
    pallas_call x1, Pallas kernels, local(): pl.pallas_call(solver_kernel, out_shape=shapes, in_specs=[hbm] * 6, out_s...  134 us

profile of v5, /device:TPU:1, one launch (start us, length us, event | category | flops | bytes accessed | tf_op | source)
XLA Modules:
  0.0 136.3 jit_solution(11916418089639903559)
XLA Ops:
  0.6 133.6 %shard_map.85 = (f32[8,256]{1,0:T(8,128)}, f32[16,8,8,256]{3,2,1,0:T(8,128)}, f32[8,256]{1,0:T(8,128)}) custom-call(f32[1,128,64,128]{3,2,1,0:T(8,128)} %stamps.1, s32[128,128]{1,0:T(8,128)} %bitcast.1, s32[1,128]{1,0:T(1,128)} %counts_in.1, f32[8,256]{1,0:T(8,128)} %cond_in.1, f32[8,256]{1,0:T(8,128)} %res_in.1, s32[16,256]{1,0:T(8,128)} %cols_in.1), custom_call_target="tpu_custom_call" | custom-call | tf_op jit(solution)/shard_map/pallas_call | solution.py:628
  134.2 2.0 %shard_map.86 = (f32[8,256]{1,0:T(8,128)}, f32[16,8,8,256]{3,2,1,0:T(8,128)}, f32[8,256]{1,0:T(8,128)}) custom-call(f32[8,256]{1,0:T(8,128)} %get-tuple-element.6.upd_in, f32[16,8,8,256]{3,2,1,0:T(8,128)} %get-tuple-element.7.jac_in, f32[8,256]{1,0:T(8,128)} %get-tuple-element.8.pre_in), custom_call_target="tpu_custom_call" | custom-call | tf_op jit(solution)/shard_map/pallas_call | solution.py:678
